TPU v7x, 256 devices: a whole 4x4x8 slice. The times are simulated.
256 devices in a mesh: row: 16 (over y_lo, x, core), col: 16 (over z, y_hi).
Axes of the slice: x: 4, y: 4 (y_hi: 2, y_lo: 2; y = y_hi * 2 + y_lo), z: 8, core: 2. Of those that a mesh axis runs over, the one named last changes fastest.
Arguments:
- query_proj: bfloat16 [32, 1024, 768], P('row', 'col'), may hold values from -16 to 16
- key_proj: bfloat16 [32, 1024, 768], P('row', 'col'), may hold values from -16 to 16
- value_proj: bfloat16 [32, 1024, 768], P('row', 'col'), may hold values from -24 to 24
- grad_output: bfloat16 [32, 1024, 768], P('row', 'col'), may hold values from -48 to 48
Outputs:
- attended: bfloat16 [32, 1024, 768], P('row', 'col')
- grad_query: bfloat16 [32, 1024, 768], P('row', 'col')
- grad_key: bfloat16 [32, 1024, 768], P('row', 'col')
- grad_value: bfloat16 [32, 1024, 768], P('row', 'col')
All inputs are finite; a program needn't handle non-finite values.
Results may differ from a plain program's by a relative error of at most 0.005.
Values may be sent and summed in bfloat16 or wider, within the bound.
A program may use at most 128 MiB of HBM per device.

v0:
```python
import math

import jax
import jax.numpy as jnp
from jax import lax
from jax.sharding import PartitionSpec as P

D = 768
H = 12


def split_heads(array):
    return array.reshape(array.shape[0], array.shape[1], H, D // H)


def shards(query_proj, key_proj, value_proj, grad_output):
    local_rows = query_proj.shape[0]
    local_cols = query_proj.shape[1]
    row_count = local_rows * lax.axis_size("row")
    factor = 1.0 / math.sqrt(D // H * row_count)
    query_heads = split_heads(query_proj)
    grad_heads = split_heads(grad_output)
    partial_value = jnp.einsum(
        "rihe,rjhe->hij",
        query_heads,
        split_heads(lax.all_gather(key_proj, "col", axis=1, tiled=True)),
        preferred_element_type=jnp.float32,
    )
    flat_partial = partial_value.reshape(H * local_cols, -1)
    logits = lax.psum(flat_partial, "row") * factor
    attn_weights = jax.nn.softmax(logits, axis=-1)
    weights_b = attn_weights.astype(jnp.bfloat16)
    weights_heads = weights_b.reshape(H, local_cols, -1)
    columns = weights_heads
    attended = jnp.einsum(
        "hij,rjhe->rihe",
        columns,
        split_heads(lax.all_gather(value_proj, "col", axis=1, tiled=True)),
        preferred_element_type=jnp.float32,
    )
    attended_out = attended.astype(jnp.bfloat16).reshape(query_proj.shape)
    dpartial = jnp.einsum(
        "rihe,rjhe->hij",
        grad_heads,
        split_heads(lax.all_gather(value_proj, "col", axis=1, tiled=True)),
        preferred_element_type=jnp.float32,
    )
    flat_dpartial = dpartial.reshape(H * local_cols, -1)
    dprobs = lax.psum(flat_dpartial, "row")
    row_dot = jnp.sum(attn_weights * dprobs, axis=-1, keepdims=True)
    dscores = (factor * attn_weights * (dprobs - row_dot)).astype(jnp.bfloat16)
    dscore_heads = dscores.reshape(H, local_cols, -1)
    columns = dscore_heads
    query_grad = jnp.einsum(
        "hij,rjhe->rihe",
        columns,
        split_heads(lax.all_gather(key_proj, "col", axis=1, tiled=True)),
        preferred_element_type=jnp.float32,
    )
    grad_query = query_grad.astype(jnp.bfloat16).reshape(query_proj.shape)
    columns = weights_heads
    stacked = lax.psum_scatter(
        jnp.stack(
            [
                jnp.einsum(
                    "hij,rihe->jrhe", dscore_heads, query_heads, preferred_element_type=jnp.float32
                ).reshape(lax.axis_size("col") * local_cols, local_rows, D),
                jnp.einsum(
                    "hij,rihe->jrhe", columns, grad_heads, preferred_element_type=jnp.float32
                ).reshape(lax.axis_size("col") * local_cols, local_rows, D),
            ],
            axis=2,
        ),
        "col",
        scatter_dimension=0,
        tiled=True,
    )
    key_grad = stacked[:, :, 0]
    value_grad = stacked[:, :, 1]
    grad_key = jnp.transpose(key_grad, (1, 0, 2)).astype(jnp.bfloat16)
    grad_value = jnp.transpose(value_grad, (1, 0, 2)).astype(jnp.bfloat16)
    return (attended_out, grad_query, grad_key, grad_value)


def solution(mesh):
    placed = (
        P("row", "col", None),
        P("row", "col", None),
        P("row", "col", None),
        P("row", "col", None),
    )
    return jax.shard_map(
        shards,
        mesh=mesh,
        in_specs=placed,
        out_specs=(
            P("row", "col", None),
            P("row", "col", None),
            P("row", "col", None),
            P("row", "col", None),
        ),
        check_vma=False,
    )
```

profile of v0, /device:TPU:8, one launch (start us, length us, event | category | flops | bytes accessed | tf_op | source)
XLA Modules:
  0.0 930.3 jit_solution(10798769900998093257)
XLA Ops:
  7.2 1.8 copy.47
  9.1 1.8 copy.51
  11.0 1.3 reshape.45
  12.7 1.3 reshape.51
  13.9 1.1 copy.61
  15.1 91.4 %all-gather.3.cloned.1.call-done = bf16[2,1024,768]{2,0,1:T(2,128)(2,1)} async-done(((bf16[2,64,768]{2,0,1:T(2,128)(2,1)}), bf16[2,1024,768]{2,0,1:T(2,128)(2,1)}) %all-gather.3.cloned.1.call-update) | async-done | bytes 3145744 | tf_op jit(solution)/shard_map/all_gather | solution.py:26
  106.5 7.0 copy.48
  113.5 2.3 fusion.6
  115.8 83.7 %all-gather.5.cloned.1.call-done = bf16[2,1024,768]{2,0,1:T(2,128)(2,1)} async-done(((bf16[2,64,768]{2,0,1:T(2,128)(2,1)}), bf16[2,1024,768]{2,0,1:T(2,128)(2,1)}) %all-gather.5.cloned.1.call-update) | async-done | bytes 3145744 | tf_op jit(solution)/shard_map/all_gather | solution.py:38
  199.5 8.7 copy.52
  208.2 4.3 fusion
  214.4 136.3 %all-reduce.5.cloned.1.call-done = (f32[768,1024]{1,0:T(8,128)}, f32[768,1024]{1,0:T(8,128)}) async-done(((f32[768,1024]{1,0:T(8,128)}, f32[768,1024]{1,0:T(8,128)}), (f32[768,1024]{1,0:T(8,128)}, f32[768,1024]{1,0:T(8,128)})) %all-reduce.5.cloned.1.call-update) | async-done | bytes 6291472 | tf_op jit(solution)/shard_map/psum | solution.py:30
  350.7 2.3 multiply_reduce_fusion.1
  355.5 2.1 multiply_convert_fusion
  357.6 1.6 fusion.16
  360.3 2.1 reshape.50
  362.4 3.0 fusion.19
  366.7 2.5 fusion.24
  369.2 1.1 copy.62
  371.6 3.2 copy.60
  374.7 9.4 %pad_maximum_fusion = f32[1024,2,2,768]{0,3,1,2:T(8,128)} fusion(f32[1024,2,1,768]{0,3,1,2:T(8,128)S(1)} %bitcast.57, f32[1024,2,1,768]{0,3,1,2:T(8,128)} %bitcast.58), kind=kLoop, calls=%fused_computation | loop fusion | flops 3145728 | bytes 25165824 | tf_op jit(solution)/shard_map/stack | solution.py:63
  384.1 19.4 %copy.63 = f32[1024,2,2,768]{3,2,1,0:T(2,128)} copy(f32[1024,2,2,768]{0,3,1,2:T(8,128)} %pad_maximum_fusion) | data formatting | bytes 25165824 | tf_op jit(solution)/shard_map/stack | solution.py:63
  403.5 518.2 %all-reduce.6 = bf16[1024,2,2,768]{3,2,1,0:T(2,128)(2,1)} all-reduce(f32[1024,2,2,768]{3,2,1,0:T(2,128)} %copy.63), channel_id=2, replica_groups=mesh['row'=16,'col'=16] {'col'}, use_global_device_ids=true, to_apply=%region_5.0.clone | all-reduce | flops 3145728 | bytes 18874368
  921.7 1.3 constant_dynamic-slice_fusion
  (28 shorter events, 8.7 us)
Async XLA Ops:
  7.2 99.3 %all-gather.3.cloned.1.call-start = ((), (), s32[]{:S(2)}) async-start(), calls=%async_computation | async-start | bytes 3342336 | tf_op jit(solution)/shard_map/all_gather | solution.py:26
  9.0 190.5 %all-gather.5.cloned.1.call-start = ((), (), s32[]{:S(2)}) async-start(), calls=%async_computation.1 | async-start | bytes 3342336 | tf_op jit(solution)/shard_map/all_gather | solution.py:38
  10.9 339.7 %all-reduce.5.cloned.1.call-start = ((), (), s32[]{:S(2)}) async-start(), calls=%async_computation.2 | async-start | bytes 12582912 | tf_op jit(solution)/shard_map/psum | solution.py:30
  212.5 0.7 copy-start.5
  350.7 2.8 copy-start
  350.7 3.8 copy-start.2
  355.4 2.2 copy-start.1
  357.6 1.7 copy-start.4
  369.2 1.4 copy-start.3
Sparse Core Ops, SparseCore 0:
  11.2 95.2 all-gather.2
  109.6 89.8 all-gather.4
  212.6 137.9 all-reduce.4
where the time goes:
time: 936 us; the launch traced here: 930 us
  blocking collectives  518 us (55%)
  waiting for transfers between devices  311 us (33%)
  local copies, waits for them, and re-layouts  55.8 us (6%)
  other arithmetic  15.5 us (2%)
  matrix products  14.7 us (2%)
  between operations  14.5 us (2%)
    unnamed x1, blocking collectives  518 us
    psum x1, waiting for transfers between devices, shards(): logits = lax.psum(flat_partial, 'row') * factor  136 us
    all_gather x1, waiting for transfers between devices, shards(): lax.all_gather(key_proj, 'col', axis=1, tiled=True)  91.4 us
    all_gather x1, waiting for transfers between devices, shards(): lax.all_gather(value_proj, 'col', axis=1, tiled=True)  83.7 us
    another operation x1, local copies, waits for them, and re-layouts, shards(): jnp.stack([jnp.einsum('hij,rihe->jrhe', dscore_heads, query_heads, prefer...  19.4 us
  transfers between devices with their start and end apart: 3, of which 3 were waited for; matrix products, arithmetic and copies ran while one was open for 2% of the time, Pallas kernels for 0%

commit v1 on v0

v1 whole, which is shorter than its diff:
```python
import functools
import math

import jax
import jax.numpy as jnp
from jax import lax
from jax.experimental import pallas as pl
from jax.experimental.pallas import tpu as pltpu
from jax.sharding import PartitionSpec as P

D = 768
H = 12
HG = 3
NX = 4
NZ = 8
C = 64
W = 512
MESH = pl.DeviceIdType.MESH
BF = jnp.bfloat16
F32 = jnp.float32


def swap_halves(first, second):
    half = first.shape[-1] // 2
    low = jnp.concatenate([first[:, :half], second[:, :half]], axis=1)
    high = jnp.concatenate([first[:, half:], second[:, half:]], axis=1)
    return low, high


def kernel(
    factor,
    q_ref, k_ref, v_ref, g_ref,
    a_out, gq_out, gk_out, gv_out,
    rep, kv, qg, part, part_in, stat, stat_in, probs, mine, eacc, edge, edge_in,
    rterm, rsend, rrecv, fin, orep,
    send_sems, recv_sems,
):
    row, col = lax.axis_index("row"), lax.axis_index("col")
    ylo, x, core = row // 8, (row // 2) % NX, row % 2
    z, yhi = col // 2, col % 2
    quarter = ylo * 2 + core

    def device(x_=None, ylo_=None, core_=None, z_=None, yhi_=None):
        x_ = x if x_ is None else x_
        ylo_ = ylo if ylo_ is None else ylo_
        core_ = core if core_ is None else core_
        z_ = z if z_ is None else z_
        yhi_ = yhi if yhi_ is None else yhi_
        return (ylo_ * 8 + x_ * 2 + core_, z_ * 2 + yhi_)

    xs = [lax.rem(x + k, NX) for k in range(NX)]
    x_peers = [device(x_=xs[k]) for k in (1, 2, 3)]
    right, left = device(z_=lax.rem(z + 1, NZ)), device(z_=lax.rem(z + NZ - 1, NZ))
    partner = device(yhi_=1 - yhi)
    group = []
    for k in (1, 2, 3):
        ylo_k, core_k = lax.rem(ylo + k // 2, 2), lax.rem(core + k % 2, 2)
        group.append((device(ylo_=ylo_k, core_=core_k), ylo_k * 2 + core_k))

    barrier = pltpu.get_barrier_semaphore()
    peers = x_peers + [right, left, partner] + [peer for peer, _ in group]
    for peer in peers:
        pl.semaphore_signal(barrier, inc=1, device_id=peer, device_id_type=MESH)

    count = [0]
    started = []

    def remote(src, dst, peer):
        index = count[0]
        count[0] += 1
        copy = pltpu.make_async_remote_copy(
            src_ref=src, dst_ref=dst, send_sem=send_sems.at[index], recv_sem=recv_sems.at[index],
            device_id=peer, device_id_type=MESH,
        )
        copy.start()
        started.append(copy)
        return copy

    def zblock(offset):
        return pl.multiple_of(lax.rem(z + offset + NZ, NZ) * C, C)

    def lanes(x_):
        return pl.ds(pl.multiple_of(x_ * 128, 128), 128)

    for array, ref in enumerate((k_ref, v_ref, q_ref, g_ref)):
        for m in range(H // 2):
            tile = slice(128 * m, 128 * m + 128)
            low, high = swap_halves(ref[0, :, tile], ref[1, :, tile])
            rep[array, 2 * m] = low
            rep[array, 2 * m + 1] = high

    pl.semaphore_wait(barrier, len(peers))

    own = pl.ds(zblock(0), C)
    ours = pl.ds(pl.multiple_of(yhi * C, C), C)
    theirs = pl.ds(pl.multiple_of((1 - yhi) * C, C), C)
    rows_q = pl.ds(pl.multiple_of(quarter * 32, 32), 32)

    kv_in, qg_in = {}, {}

    def x_in(h):
        kv_in[h] = [
            remote(rep.at[pl.ds(0, 2), xs[k] * HG + h], kv.at[:, h, own, lanes(x)], x_peers[k - 1])
            for k in (1, 2, 3)
        ]
        qg_in[h] = [
            remote(rep.at[pl.ds(2, 2), xs[k] * HG + h], qg.at[:, h, ours, lanes(x)], x_peers[k - 1])
            for k in (1, 2, 3)
        ]
        for t in range(2):
            kv[t, h, own, lanes(x)] = rep[t, x * HG + h]
            qg[t, h, ours, lanes(x)] = rep[2 + t, x * HG + h]

    ring = {}

    def ag_send(h, t, step):
        full = step < 4
        right_block = zblock(1 - step)
        left_block = zblock(step - 1)
        size = C if full else C // 2
        there = kv.at[t, h, pl.ds(right_block, size)]
        back = kv.at[t, h, pl.ds(left_block if full else left_block + C // 2, size)]
        ring[h, t, step] = (remote(there, there, right), remote(back, back, left))

    def ag_start(h):
        for copy in kv_in[h]:
            copy.wait_recv()
        for t in range(2):
            ag_send(h, t, 1)

    def ag_step(h, step):
        for t in range(2):
            for copy in ring[h, t, step]:
                copy.wait_recv()
            if step < 4:
                ag_send(h, t, step + 1)

    qg_swap = {}

    def qg_start(h):
        for copy in qg_in[h]:
            copy.wait_recv()
        half = qg.at[:, h, ours]
        qg_swap[h] = remote(half, half, partner)

    part_copies = {}

    def s_compute(h):
        qg_swap[h].wait_recv()
        for t in range(2):
            part[t, h] = lax.dot_general(
                qg[t, h], kv[t, h], (((1,), (1,)), ((), ())), preferred_element_type=F32
            )
        part_copies[h] = [
            remote(
                part.at[:, h, pl.ds(pl.multiple_of(theirs_q * 32, 32), 32)], part_in.at[:, h, k], peer
            )
            for k, (peer, theirs_q) in enumerate(group)
        ]

    stat_copies = {}

    def s_reduce(h):
        for copy in part_copies[h]:
            copy.wait_recv()
        score, dprob = (
            (part[t, h, rows_q] + part_in[t, h, 0]) + (part_in[t, h, 1] + part_in[t, h, 2])
            for t in range(2)
        )
        score = score * factor
        top = jnp.max(score, axis=1, keepdims=True)
        weight = jnp.exp(score - top)
        total = jnp.sum(weight, axis=1, keepdims=True)
        dot = jnp.sum(weight * dprob, axis=1, keepdims=True)
        mine[0, h] = weight
        mine[1, h] = dprob
        lane = lax.broadcasted_iota(jnp.int32, (32, 128), 1)
        stat[h] = jnp.where(lane == 0, top, jnp.where(lane == 1, total, dot))
        stat_copies[h] = remote(stat.at[h], stat_in.at[h], partner)

    probs_copies = {}

    def p_compute(h):
        stat_copies[h].wait_recv()
        here, there = stat[h], stat_in[h]
        top_a, total_a, dot_a = here[:, 0:1], here[:, 1:2], here[:, 2:3]
        top_b, total_b, dot_b = there[:, 0:1], there[:, 1:2], there[:, 2:3]
        top = jnp.maximum(top_a, top_b)
        scale_a, scale_b = jnp.exp(top_a - top), jnp.exp(top_b - top)
        total = total_a * scale_a + total_b * scale_b
        row_dot = (dot_a * scale_a + dot_b * scale_b) / total
        weights = mine[0, h] * (scale_a / total)
        probs[0, h, rows_q] = weights.astype(BF)
        probs[1, h, rows_q] = (factor * weights * (mine[1, h] - row_dot)).astype(BF)
        block = probs.at[:, h, rows_q]
        probs_copies[h] = [remote(block, block, peer) for peer, _ in group]

    edge_copies = {}
    sums = {}

    def rs_send(h, t, step):
        for way, peer in ((0, right), (1, left)):
            offset = (5 - step) * (1 if way == 0 else -1)
            start = zblock(offset)
            if step == 1:
                half = C // 2 * way
                rsend[t, h, way, 0, half : half + C // 2] = rterm[
                    t, h, pl.ds(start + half, C // 2)
                ].astype(BF)
                src, dst = (
                    ref.at[t, h, way, 0, pl.ds(half, C // 2)] for ref in (rsend, rrecv)
                )
            else:
                sums[h, t, step - 1][way].wait_recv()
                term = rterm[t, h, pl.ds(start, C)]
                if step == 2:
                    half = C // 2 * way
                    other = C // 2 - half
                    rsend[t, h, way, 1, half : half + C // 2] = (
                        rterm[t, h, pl.ds(start + half, C // 2)]
                        + rrecv[t, h, way, 0, half : half + C // 2].astype(F32)
                    ).astype(BF)
                    rsend[t, h, way, 1, other : other + C // 2] = rterm[
                        t, h, pl.ds(start + other, C // 2)
                    ].astype(BF)
                else:
                    rsend[t, h, way, step - 1] = (
                        term + rrecv[t, h, way, step - 2].astype(F32)
                    ).astype(BF)
                src, dst = rsend.at[t, h, way, step - 1], rrecv.at[t, h, way, step - 1]
            sums.setdefault((h, t, step), []).append(remote(src, dst, peer))

    def out_compute(h):
        for copy in probs_copies[h]:
            copy.wait_recv()
        for t, (p, other) in enumerate(((1, 0), (0, 1))):
            rterm[t, h] = lax.dot_general(
                probs[p, h], qg[other, h], (((0,), (0,)), ((), ())), preferred_element_type=F32
            )
            rs_send(h, t, 1)
        for t, (p, other) in enumerate(((0, 1), (1, 0))):
            eacc[t, h] = jnp.dot(probs[p, h], kv[other, h], preferred_element_type=F32)
            edge[t, h] = eacc[t, h, theirs].astype(BF)
        edge_copies[h] = remote(edge.at[:, h], edge_in.at[:, h], partner)

    out_copies = []

    def x_out(h, first):
        out_copies.extend(
            remote(
                fin.at[pl.ds(first, 2), h, :, lanes(xs[k])],
                orep.at[pl.ds(first, 2), x * HG + h],
                x_peers[k - 1],
            )
            for k in (1, 2, 3)
        )
        for t in range(2):
            orep[first + t, x * HG + h] = fin[first + t, h, :, lanes(x)]

    def edge_end(h):
        edge_copies[h].wait_recv()
        for t in range(2):
            fin[t, h] = (eacc[t, h, ours] + edge_in[t, h].astype(F32)).astype(BF)
        x_out(h, 0)

    def rs_step(h, step):
        for t in range(2):
            rs_send(h, t, step)

    def rs_end(h):
        for t in range(2):
            for copy in sums[h, t, 4]:
                copy.wait_recv()
            fin[2 + t, h] = (
                rterm[t, h, own]
                + (rrecv[t, h, 0, 3].astype(F32) + rrecv[t, h, 1, 3].astype(F32))
            ).astype(BF)
        x_out(h, 2)

    for h in range(HG):
        x_in(h)
    ag_start(0)
    qg_start(0)
    ag_step(0, 1)
    ag_step(0, 2)
    ag_start(1)
    qg_start(1)
    ag_step(0, 3)
    ag_step(1, 1)
    ag_step(0, 4)
    s_compute(0)
    ag_step(1, 2)
    ag_start(2)
    qg_start(2)
    s_reduce(0)
    ag_step(1, 3)
    p_compute(0)
    ag_step(2, 1)
    ag_step(1, 4)
    s_compute(1)
    ag_step(2, 2)
    out_compute(0)
    s_reduce(1)
    ag_step(2, 3)
    p_compute(1)
    rs_step(0, 2)
    edge_end(0)
    ag_step(2, 4)
    s_compute(2)
    out_compute(1)
    rs_step(0, 3)
    s_reduce(2)
    rs_step(1, 2)
    rs_step(0, 4)
    p_compute(2)
    edge_end(1)
    rs_step(1, 3)
    out_compute(2)
    rs_end(0)
    rs_step(1, 4)
    rs_step(2, 2)
    edge_end(2)
    rs_end(1)
    rs_step(2, 3)
    rs_step(2, 4)
    rs_end(2)

    for copy in out_copies:
        copy.wait_recv()
    for array, ref in enumerate((a_out, gq_out, gk_out, gv_out)):
        for m in range(H // 2):
            tile = slice(128 * m, 128 * m + 128)
            first, second = swap_halves(orep[array, 2 * m], orep[array, 2 * m + 1])
            ref[0, :, tile] = first
            ref[1, :, tile] = second
    for copy in started:
        copy.wait_send()


COPIES = 18 + 48 + 3 + 9 + 3 + 9 + 3 + 48 + 18


def shards(query_proj, key_proj, value_proj, grad_output):
    row_count = query_proj.shape[0] * lax.axis_size("row")
    factor = 1.0 / math.sqrt(D // H * row_count)
    vmem = pl.BlockSpec(memory_space=pltpu.VMEM)
    shape = jax.ShapeDtypeStruct(query_proj.shape, BF)
    return pl.pallas_call(
        functools.partial(kernel, factor),
        out_shape=(shape,) * 4,
        in_specs=[vmem] * 4,
        out_specs=(vmem,) * 4,
        scratch_shapes=[
            pltpu.VMEM((4, H, C, 128), BF),
            pltpu.VMEM((2, HG, NZ * C, W), BF),
            pltpu.VMEM((2, HG, 2 * C, W), BF),
            pltpu.VMEM((2, HG, 2 * C, W), F32),
            pltpu.VMEM((2, HG, 3, 32, W), F32),
            pltpu.VMEM((HG, 32, 128), F32),
            pltpu.VMEM((HG, 32, 128), F32),
            pltpu.VMEM((2, HG, 2 * C, W), BF),
            pltpu.VMEM((2, HG, 32, W), F32),
            pltpu.VMEM((2, HG, 2 * C, W), F32),
            pltpu.VMEM((2, HG, C, W), BF),
            pltpu.VMEM((2, HG, C, W), BF),
            pltpu.VMEM((2, HG, NZ * C, W), F32),
            pltpu.VMEM((2, HG, 2, 4, C, W), BF),
            pltpu.VMEM((2, HG, 2, 4, C, W), BF),
            pltpu.VMEM((4, HG, C, W), BF),
            pltpu.VMEM((4, H, C, 128), BF),
            pltpu.SemaphoreType.DMA((COPIES,)),
            pltpu.SemaphoreType.DMA((COPIES,)),
        ],
        compiler_params=pltpu.CompilerParams(
            collective_id=0, has_side_effects=True, vmem_limit_bytes=56 * 2**20
        ),
        cost_estimate=pl.CostEstimate(flops=1_208_000_000, bytes_accessed=1_600_000, transcendentals=50_000),
    )(query_proj, key_proj, value_proj, grad_output)


def solution(mesh):
    placed = P("row", "col", None)
    return jax.shard_map(
        shards,
        mesh=mesh,
        in_specs=(placed,) * 4,
        out_specs=(placed,) * 4,
        check_vma=False,
    )
```

time: 936 us -> 106 us (0.11)
  blocking collectives: 518 us -> 0 us
  waiting for transfers between devices: 311 us -> 0 us
  Pallas kernels: 0 us -> 101 us
  local copies, waits for them, and re-layouts: 55.8 us -> 4.33 us
  other arithmetic: 15.5 us -> 0 us
  matrix products: 14.7 us -> 0 us
  between operations: 14.5 us -> 0.65 us
    unnamed x1 -> x0, blocking collectives: 518 us -> none
    all_gather x2 -> x0, waiting for transfers between devices: 175 us -> none  [the longest x1 91.4 us: shards(): lax.all_gather(key_proj, 'col', axis=1, tiled=True)]
    psum x1 -> x0, waiting for transfers between devices: 136 us -> none  [shards(): logits = lax.psum(flat_partial, 'row') * factor]
    pallas_call x0 -> x1, Pallas kernels: none -> 101 us  [shards(): pl.pallas_call(functools.partial(kernel, factor), out_shape=(shape,) * 4,...]
    another operation x1 -> x0, local copies, waits for them, and re-layouts: 19.4 us -> none  [shards(): jnp.stack([jnp.einsum('hij,rihe->jrhe', dscore_heads, query_heads, prefer...]
    all_gather x2 -> x0, local copies, waits for them, and re-layouts: 15.7 us -> none  [the longest x1 8.65 us: shards(): lax.all_gather(value_proj, 'col', axis=1, tiled=True)]
    dot_general x4 -> x0, matrix products: 11.3 us -> none  [the longest x1 4.31 us: shards(): jnp.einsum('rihe,rjhe->hij', grad_heads, split_heads(lax.all_gather(value...]
    another operation x1 -> x0, other arithmetic: 9.38 us -> none  [shards(): jnp.stack([jnp.einsum('hij,rihe->jrhe', dscore_heads, query_heads, prefer...]
  transfers between devices with their start and end apart: 3 -> 0, of which waited for: 3 -> 0; matrix products, arithmetic and copies ran while one was open for 2% -> 0% of each run, Pallas kernels for 0% -> 0%
where the time goes in v1:
time: 106 us
  Pallas kernels  101 us (95%)
  local copies, waits for them, and re-layouts  4.33 us (4%)
    pallas_call x1, Pallas kernels, shards(): pl.pallas_call(functools.partial(kernel, factor), out_shape=(shape,) * 4,...  101 us
    unnamed x10, local copies, waits for them, and re-layouts  4.33 us

profile of v1, /device:TPU:8, one launch (start us, length us, event | category | flops | bytes accessed | tf_op | source)
XLA Modules:
  0.0 105.7 jit_solution(5531298303190891899)
XLA Ops:
  0.6 100.8 %shard_map.75 = (bf16[2,64,768]{2,1,0:T(8,128)(2,1)}, bf16[2,64,768]{2,1,0:T(8,128)(2,1)}, bf16[2,64,768]{2,1,0:T(8,128)(2,1)}, bf16[2,64,768]{2,1,0:T(8,128)(2,1)}) custom-call(bf16[2,64,768]{2,1,0:T(8,128)(2,1)} %q_ref.1, bf16[2,64,768]{2,1,0:T(8,128)(2,1)} %k_ref.1, bf16[2,64,768]{2,1,0:T(8,128)(2,1)} %v_ref.1, bf16[2,64,768]{2,1,0:T(8,128)(2,1)} %g_ref.1), custom_call_target="tpu_custom_call" | custom-call | flops 1208000000 | bytes 1600000 | tf_op jit(solution)/shard_map/pallas_call | solution.py:348
  101.4 0.0 copy-start.2
  101.4 1.7 %copy.12 = bf16[2,64,768]{2,1,0:T(8,128)(2,1)} copy(bf16[2,64,768]{2,1,0:T(8,128)(2,1)} %get-tuple-element.8) | data formatting | bytes 393216
  103.1 0.0 copy-done.2
  103.1 0.0 copy-start.1
  103.1 0.7 copy.13
  103.8 0.3 copy-done.1
  104.1 0.0 copy-start
  104.1 0.7 copy.14
  104.8 0.3 copy-done
  105.1 0.7 copy.15
Async XLA Ops:
  101.4 1.7 %copy-start.2 = (bf16[2,64,768]{2,1,0:T(8,128)(2,1)S(1)}, bf16[2,64,768]{2,1,0:T(8,128)(2,1)}, u32[]{:S(2)}) copy-start(bf16[2,64,768]{2,1,0:T(8,128)(2,1)} %get-tuple-element.9) | copy-start | bytes 589828
  103.1 1.0 copy-start.1
  104.1 1.0 copy-start

commit v2 on v0

v2 whole, which is shorter than its diff:
```python
import functools
import math

import jax
import jax.numpy as jnp
from jax import lax
from jax.experimental import pallas as pl
from jax.experimental.pallas import tpu as pltpu
from jax.sharding import PartitionSpec as P

D = 768
H = 12
NX = 4
NZ = 8
C = 64
W = 512
J = 512
MESH = pl.DeviceIdType.MESH
BF = jnp.bfloat16
F32 = jnp.float32

ATTENDED, GRAD_QUERY, GRAD_KEY, GRAD_VALUE = range(4)


def swap_halves(first, second):
    half = first.shape[-1] // 2
    low = jnp.concatenate([first[:, :half], second[:, :half]], axis=1)
    high = jnp.concatenate([first[:, half:], second[:, half:]], axis=1)
    return low, high


def nt_dot(a, b):
    return lax.dot_general(a, b, (((1,), (1,)), ((), ())), preferred_element_type=F32)


def tn_dot(a, b):
    return lax.dot_general(a, b, (((0,), (0,)), ((), ())), preferred_element_type=F32)


class Unit:
    def __init__(self, net, n, cb, me, right, left, refs):
        self.net, self.n, self.cb, self.me = net, n, cb, me
        self.right, self.left = right, left
        (
            self.kv, self.qg, self.part, self.core_in, self.half, self.ylo_in, self.stat, self.stat_in,
            self.probs, self.mine, self.eacc, self.edge, self.edge_in, self.rterm, self.rsend,
            self.rrecv, self.fin,
        ) = refs
        self.ours = pl.ds(pl.multiple_of(net.yhi * cb, cb), cb)
        self.theirs = pl.ds(pl.multiple_of((1 - net.yhi) * cb, cb), cb)
        self.own = pl.ds(self.block(0), cb)
        self.quarter = cb // 2
        self.rows_q = pl.ds(
            pl.multiple_of(net.core * cb + net.ylo * self.quarter, self.quarter), self.quarter
        )
        self.ring, self.swap, self.core_copy, self.ylo_copy = {}, {}, {}, {}
        self.stat_copy, self.probs_copy, self.edge_copy, self.sums = {}, {}, {}, {}

    @staticmethod
    def scratch(n, cb):
        return [
            pltpu.VMEM((2, J, W), BF),
            pltpu.VMEM((2, 2 * cb, W), BF),
            pltpu.VMEM((2, 2 * cb, J), F32),
            pltpu.VMEM((2, cb, J), F32),
            pltpu.VMEM((2, cb, J), F32),
            pltpu.VMEM((2, cb // 2, J), F32),
            pltpu.VMEM((2, cb // 2, 128), F32),
            pltpu.VMEM((2, cb // 2, 128), F32),
            pltpu.VMEM((2, 2 * cb, J), BF),
            pltpu.VMEM((2, cb // 2, J), F32),
            pltpu.VMEM((2, 2 * cb, W), F32),
            pltpu.VMEM((2, cb, W), BF),
            pltpu.VMEM((2, cb, W), BF),
            pltpu.VMEM((2, J, W), F32),
            pltpu.VMEM((2, 2, n // 2, cb, W), BF),
            pltpu.VMEM((2, 2, n // 2, cb, W), BF),
            pltpu.VMEM((4, cb, W), BF),
        ]

    def block(self, offset):
        return pl.multiple_of(lax.rem(self.me + offset + self.n, self.n) * self.cb, self.cb)

    def ring_send(self, t, step):
        full = step < self.n // 2
        size = self.cb if full else self.cb // 2
        left_block = self.block(step - 1)
        there = self.kv.at[t, pl.ds(self.block(1 - step), size)]
        back = self.kv.at[t, pl.ds(left_block if full else left_block + self.cb // 2, size)]
        self.ring[t, step] = (
            self.net.remote(there, there, self.right),
            self.net.remote(back, back, self.left),
        )

    def ring_step(self, t, step):
        for copy in self.ring[t, step]:
            copy.wait_recv()
        if step < self.n // 2:
            self.ring_send(t, step + 1)

    def swap_start(self, t):
        mine = self.qg.at[t, self.ours]
        self.swap[t] = self.net.remote(mine, mine, self.net.partner)

    def s_compute(self, t):
        self.swap[t].wait_recv()
        self.part[t] = nt_dot(self.qg[t], self.kv[t])
        other = pl.ds(pl.multiple_of((1 - self.net.core) * self.cb, self.cb), self.cb)
        self.core_copy[t] = self.net.remote(
            self.part.at[t, other], self.core_in.at[t], self.net.core_peer
        )

    def s_core(self, t):
        self.core_copy[t].wait_recv()
        rows = pl.ds(pl.multiple_of(self.net.core * self.cb, self.cb), self.cb)
        self.half[t] = self.part[t, rows] + self.core_in[t]
        other = pl.ds(
            pl.multiple_of((1 - self.net.ylo) * self.quarter, self.quarter), self.quarter
        )
        self.ylo_copy[t] = self.net.remote(
            self.half.at[t, other], self.ylo_in.at[t], self.net.ylo_peer
        )

    def s_reduce(self, t):
        self.ylo_copy[t].wait_recv()
        rows = pl.ds(pl.multiple_of(self.net.ylo * self.quarter, self.quarter), self.quarter)
        total = self.half[t, rows] + self.ylo_in[t]
        if t == 0:
            score = total * self.net.factor
            top = jnp.max(score, axis=1, keepdims=True)
            weight = jnp.exp(score - top)
            self.mine[0] = weight
            lane = lax.broadcasted_iota(jnp.int32, (self.quarter, 128), 1)
            self.stat[0] = jnp.where(lane == 0, top, jnp.sum(weight, axis=1, keepdims=True))
        else:
            self.mine[1] = total
            dot = jnp.sum(self.mine[0] * total, axis=1, keepdims=True)
            self.stat[1] = jnp.broadcast_to(dot, (self.quarter, 128))
        self.stat_copy[t] = self.net.remote(
            self.stat.at[t], self.stat_in.at[t], self.net.partner
        )

    def p_compute(self, t):
        self.stat_copy[t].wait_recv()
        here, there = self.stat[t], self.stat_in[t]
        if t == 0:
            top_a, top_b = here[:, 0:1], there[:, 0:1]
            top = jnp.maximum(top_a, top_b)
            scale_a, scale_b = jnp.exp(top_a - top), jnp.exp(top_b - top)
            total = here[:, 1:2] * scale_a + there[:, 1:2] * scale_b
            weights = self.mine[0] * (scale_a / total)
            self.mine[0] = weights
            self.probs[0, self.rows_q] = weights.astype(BF)
        else:
            row_dot = here[:, 0:1] + there[:, 0:1]
            self.probs[1, self.rows_q] = (
                self.net.factor * self.mine[0] * (self.mine[1] - row_dot)
            ).astype(BF)
        block = self.probs.at[t, self.rows_q]
        self.probs_copy[t] = [
            self.net.remote(block, block, peer)
            for peer in (self.net.ylo_peer, self.net.far_peer, self.net.core_peer)
        ]

    def out_compute(self, t):
        for copy in self.probs_copy[t]:
            copy.wait_recv()
        self.rterm[t] = tn_dot(self.probs[t], self.qg[1 - t])
        self.rs_send(t, 1)
        self.eacc[t] = jnp.dot(self.probs[t], self.kv[1 - t], preferred_element_type=F32)
        self.edge[t] = self.eacc[t, self.theirs].astype(BF)
        self.edge_copy[t] = self.net.remote(
            self.edge.at[t], self.edge_in.at[t], self.net.partner
        )

    def rs_send(self, t, step):
        cb, half = self.cb, self.cb // 2
        for way, peer in ((0, self.right), (1, self.left)):
            start = self.block((self.n // 2 + 1 - step) * (1 if way == 0 else -1))
            first, rest = slice(half * way, half * way + half), slice(half - half * way, cb - half * way)
            send = self.rsend.at[t, way, step - 1]
            recv = self.rrecv.at[t, way, step - 1]
            if step == 1:
                send[first] = self.rterm[t, pl.ds(start + half * way, half)].astype(BF)
                send, recv = (ref.at[pl.ds(half * way, half)] for ref in (send, recv))
            else:
                self.sums[t, step - 1][way].wait_recv()
                arrived = self.rrecv.at[t, way, step - 2]
                if step == 2:
                    send[first] = (
                        self.rterm[t, pl.ds(start + half * way, half)] + arrived[first].astype(F32)
                    ).astype(BF)
                    send[rest] = self.rterm[t, pl.ds(start + half - half * way, half)].astype(BF)
                else:
                    send[...] = (
                        self.rterm[t, pl.ds(start, cb)] + arrived[...].astype(F32)
                    ).astype(BF)
            self.sums.setdefault((t, step), []).append(self.net.remote(send, recv, peer))

    def rs_end(self, t):
        last = self.n // 2
        for copy in self.sums[t, last]:
            copy.wait_recv()
        index = (GRAD_VALUE, GRAD_KEY)[t]
        self.fin[index] = (
            self.rterm[t, self.own]
            + (self.rrecv[t, 0, last - 1].astype(F32) + self.rrecv[t, 1, last - 1].astype(F32))
        ).astype(BF)
        self.out_send(index)

    def edge_end(self, t):
        self.edge_copy[t].wait_recv()
        index = (ATTENDED, GRAD_QUERY)[t]
        self.fin[index] = (
            self.eacc[t, self.ours] + self.edge_in[t].astype(F32)
        ).astype(BF)
        self.out_send(index)


class XUnit(Unit):
    def in_send(self, t):
        net = self.net
        lanes = net.lanes(net.x)
        self.arrive = getattr(self, "arrive", {})
        for name, array, ref, rows in ((0, t, self.kv, self.own), (1, 2 + t, self.qg, self.ours)):
            self.arrive[name, t] = [
                net.remote(net.rep.at[array, NZ + net.xs[k]], ref.at[t, rows, lanes], net.x_peers[k])
                for k in (2, 1, 3)
            ]
            ref[t, rows, lanes] = net.rep[array, NZ + net.x]

    def in_wait(self, name, t):
        for copy in self.arrive[name, t]:
            copy.wait_recv()

    def out_send(self, index):
        net = self.net
        self.leave = getattr(self, "leave", {})
        self.leave[index] = [
            net.remote(
                self.fin.at[index, :, net.lanes(net.xs[k])], net.orep.at[index, NZ + net.x], net.x_peers[k]
            )
            for k in (2, 1, 3)
        ]
        net.orep[index, NZ + net.x] = self.fin[index, :, net.lanes(net.x)]

    def out_wait(self, index):
        for copy in self.leave[index]:
            copy.wait_recv()


class ZUnit(Unit):
    def in_send(self, t):
        net = self.net
        lanes = net.lanes(net.x)
        self.arrive = getattr(self, "arrive", {})
        slot = net.x * 2 + lax.rem(net.z, 2)
        sub = lax.rem(net.z, 2) * C
        bases = [net.take(NZ), net.take(NZ)]
        for k in (4, 3, 5, 2, 6, 1, 7, 0):
            z_to = lax.rem(net.z + k, NZ)
            x_to = lax.rem(net.z // 2 + z_to, NX)
            alone = None if k else x_to == net.x
            for name, array, ref, start in (
                (0, t, self.kv, x_to * self.cb),
                (1, 2 + t, self.qg, net.yhi * self.cb),
            ):
                dst = ref.at[t, pl.ds(pl.multiple_of(start + sub, C), C), lanes]
                net.remote(
                    net.rep.at[array, z_to], dst, net.device(x=x_to, z=z_to),
                    recv=bases[name] + slot, alone=alone,
                )
        for name, ref in ((0, self.kv), (1, self.qg)):
            self.arrive[name, t] = [
                (ref.at[t, pl.ds(0, C), pl.ds(0, 128)], bases[name] + k) for k in range(NZ)
            ]

    def in_wait(self, name, t):
        for ref, index in self.arrive[name, t]:
            self.net.wait_recv(ref, index)

    def out_send(self, index):
        net = self.net
        self.leave = getattr(self, "leave", {})
        pair = lax.rem(net.x - net.z + NZ, NX)
        base = net.take(NZ)
        for k in (2, 1, 3, 0):
            for s in range(2):
                z_to = pair * 2 + s
                net.remote(
                    self.fin.at[index, pl.ds(s * C, C), net.lanes(net.xs[k])],
                    net.orep.at[index, net.z],
                    net.device(x=net.xs[k], z=z_to),
                    recv=base + net.z, alone=None if k else z_to == net.z,
                )
        self.leave[index] = [(net.orep.at[index, k], base + k) for k in range(NZ)]

    def out_wait(self, index):
        for ref, slot in self.leave[index]:
            self.net.wait_recv(ref, slot)


class Net:
    def __init__(self, factor, rep, orep, send_sems, recv_sems):
        self.factor, self.rep, self.orep = factor, rep, orep
        self.send_sems, self.recv_sems = send_sems, recv_sems
        row, col = lax.axis_index("row"), lax.axis_index("col")
        self.ylo, self.x, self.core = row // 8, lax.rem(row // 2, NX), lax.rem(row, 2)
        self.z, self.yhi = col // 2, lax.rem(col, 2)
        self.xs = [lax.rem(self.x + k, NX) for k in range(NX)]
        self.x_peers = [self.device(x=x) for x in self.xs]
        self.partner = self.device(yhi=1 - self.yhi)
        self.core_peer = self.device(core=1 - self.core)
        self.ylo_peer = self.device(ylo=1 - self.ylo)
        self.far_peer = self.device(ylo=1 - self.ylo, core=1 - self.core)
        self.sent, self.received, self.started = 0, 0, []

    def device(self, **at):
        ylo, x, core, z, yhi = (at.get(k, getattr(self, k)) for k in ("ylo", "x", "core", "z", "yhi"))
        return (ylo * 8 + x * 2 + core, z * 2 + yhi)

    def lanes(self, x):
        return pl.ds(pl.multiple_of(x * 128, 128), 128)

    def take(self, n):
        self.received += n
        return self.received - n

    def remote(self, src, dst, peer, recv=None, alone=None):
        recv = self.take(1) if recv is None else recv
        send = self.send_sems.at[self.sent]
        self.sent += 1
        copy = pltpu.make_async_remote_copy(
            src_ref=src, dst_ref=dst, send_sem=send, recv_sem=self.recv_sems.at[recv],
            device_id=peer, device_id_type=MESH,
        )
        if alone is None:
            copy.start()
        else:
            pl.when(jnp.logical_not(alone))(copy.start)
            pl.when(alone)(pltpu.make_async_copy(src, dst, self.recv_sems.at[recv]).start)
        self.started.append((copy, alone))
        return copy

    def wait_recv(self, ref, index):
        pltpu.make_async_copy(ref, ref, self.recv_sems.at[index]).wait()

    def finish(self):
        for copy, alone in self.started:
            if alone is None:
                copy.wait_send()
            else:
                pl.when(jnp.logical_not(alone))(copy.wait_send)


def kernel(factor, q_ref, k_ref, v_ref, g_ref, orep, rep, send_sems, recv_sems, *refs):
    net = Net(factor, rep, orep, send_sems, recv_sems)
    count = len(refs) // 2
    small = XUnit(
        net, NZ, C, net.z,
        net.device(z=lax.rem(net.z + 1, NZ)), net.device(z=lax.rem(net.z + NZ - 1, NZ)), refs[:count],
    )
    big = ZUnit(net, NX, 2 * C, net.x, net.x_peers[1], net.x_peers[3], refs[count:])

    barrier = pltpu.get_barrier_semaphore()

    def greet(peer):
        pl.semaphore_signal(barrier, inc=1, device_id=peer, device_id_type=MESH)

    near = net.x_peers[1:] + [small.right, small.left, net.partner, net.core_peer, net.ylo_peer, net.far_peer]
    pair = lax.rem(net.x - net.z + NZ, NX)
    for k in (2, 1, 3, 0):
        for s in range(2):
            peer = net.device(x=net.xs[k], z=pair * 2 + s)
            if k:
                greet(peer)
            else:
                pl.when(pair * 2 + s != net.z)(functools.partial(greet, peer))
    for peer in near:
        greet(peer)

    for array, ref in ((0, k_ref), (2, q_ref), (1, v_ref), (3, g_ref)):
        for m in range(H // 2):
            tile = slice(128 * m, 128 * m + 128)
            low, high = swap_halves(ref[0, :, tile], ref[1, :, tile])
            rep[array, 2 * m] = low
            rep[array, 2 * m + 1] = high

    alone = (lax.rem(net.z // 2 + net.z, NX) == net.x).astype(jnp.int32)
    pl.semaphore_wait(barrier, len(near) + NZ - alone)

    for t in range(2):
        small.in_send(t)
        big.in_send(t)

    def ring_start(unit, t):
        unit.in_wait(0, t)
        unit.ring_send(t, 1)

    def swap_start(unit, t):
        unit.in_wait(1, t)
        unit.swap_start(t)

    ring_start(small, 0)
    swap_start(small, 0)
    ring_start(small, 1)
    swap_start(small, 1)
    ring_start(big, 0)
    swap_start(big, 0)
    small.ring_step(0, 1)
    small.ring_step(1, 1)
    small.ring_step(0, 2)
    ring_start(big, 1)
    swap_start(big, 1)
    big.ring_step(0, 1)
    small.ring_step(1, 2)
    small.ring_step(0, 3)
    big.ring_step(0, 2)
    big.s_compute(0)
    small.ring_step(1, 3)
    big.ring_step(1, 1)
    big.s_core(0)
    small.ring_step(0, 4)
    small.s_compute(0)
    small.ring_step(1, 4)
    small.s_core(0)
    big.ring_step(1, 2)
    big.s_compute(1)
    small.s_compute(1)
    big.s_core(1)
    small.s_core(1)
    big.s_reduce(0)
    small.s_reduce(0)
    big.p_compute(0)
    small.p_compute(0)
    big.s_reduce(1)
    small.s_reduce(1)
    big.out_compute(0)
    small.out_compute(0)
    big.p_compute(1)
    small.p_compute(1)
    big.rs_send(0, 2)
    small.rs_send(0, 2)
    big.out_compute(1)
    small.out_compute(1)
    small.rs_send(0, 3)
    big.edge_end(0)
    small.edge_end(0)
    big.rs_end(0)
    small.rs_send(1, 2)
    big.rs_send(1, 2)
    small.rs_send(0, 4)
    small.rs_send(1, 3)
    big.edge_end(1)
    small.edge_end(1)
    big.rs_end(1)
    small.rs_end(0)
    small.rs_send(1, 4)
    small.rs_end(1)

    for unit in (big, small):
        for index in range(4):
            unit.out_wait(index)
    net.finish()


def repack(orep, *outs):
    for array, ref in enumerate(outs):
        for m in range(H // 2):
            tile = slice(128 * m, 128 * m + 128)
            first, second = swap_halves(orep[array, 2 * m], orep[array, 2 * m + 1])
            ref[0, :, tile] = first
            ref[1, :, tile] = second


COPIES = 180


def shards(query_proj, key_proj, value_proj, grad_output):
    row_count = query_proj.shape[0] * lax.axis_size("row")
    factor = 1.0 / math.sqrt(D // H * row_count)
    vmem = pl.BlockSpec(memory_space=pltpu.VMEM)
    blocks = pl.pallas_call(
        functools.partial(kernel, factor),
        out_shape=jax.ShapeDtypeStruct((4, H, C, 128), BF),
        in_specs=[vmem] * 4,
        out_specs=vmem,
        scratch_shapes=[
            pltpu.VMEM((4, H, C, 128), BF),
            pltpu.SemaphoreType.DMA((COPIES,)),
            pltpu.SemaphoreType.DMA((COPIES,)),
            *Unit.scratch(NZ, C),
            *Unit.scratch(NX, 2 * C),
        ],
        compiler_params=pltpu.CompilerParams(
            collective_id=0, has_side_effects=True, vmem_limit_bytes=48 * 2**20
        ),
        cost_estimate=pl.CostEstimate(flops=1_208_000_000, bytes_accessed=1_600_000, transcendentals=50_000),
        name="exchange_and_compute",
    )(query_proj, key_proj, value_proj, grad_output)
    return pl.pallas_call(
        repack,
        out_shape=(jax.ShapeDtypeStruct(query_proj.shape, BF),) * 4,
        in_specs=[vmem],
        out_specs=(vmem,) * 4,
        name="repack",
    )(blocks)


def solution(mesh):
    placed = P("row", "col", None)
    return jax.shard_map(
        shards,
        mesh=mesh,
        in_specs=(placed,) * 4,
        out_specs=(placed,) * 4,
        check_vma=False,
    )
```

time: 936 us -> 106 us (0.11)
  blocking collectives: 518 us -> 0 us
  waiting for transfers between devices: 311 us -> 0 us
  Pallas kernels: 0 us -> 100 us
  local copies, waits for them, and re-layouts: 55.8 us -> 4.58 us
  other arithmetic: 15.5 us -> 0 us
  matrix products: 14.7 us -> 0 us
  between operations: 14.5 us -> 0.66 us
    unnamed x1 -> x0, blocking collectives: 518 us -> none
    all_gather x2 -> x0, waiting for transfers between devices: 175 us -> none  [the longest x1 91.4 us: shards(): lax.all_gather(key_proj, 'col', axis=1, tiled=True)]
    psum x1 -> x0, waiting for transfers between devices: 136 us -> none  [shards(): logits = lax.psum(flat_partial, 'row') * factor]
    pallas_call x0 -> x2, Pallas kernels: none -> 100 us  [the longest x1 98.4 us: shards(): pl.pallas_call(functools.partial(kernel, factor), out_shape=jax.ShapeDtyp...]
    another operation x1 -> x0, local copies, waits for them, and re-layouts: 19.4 us -> none  [shards(): jnp.stack([jnp.einsum('hij,rihe->jrhe', dscore_heads, query_heads, prefer...]
    all_gather x2 -> x0, local copies, waits for them, and re-layouts: 15.7 us -> none  [the longest x1 8.65 us: shards(): lax.all_gather(value_proj, 'col', axis=1, tiled=True)]
    dot_general x4 -> x0, matrix products: 11.3 us -> none  [the longest x1 4.31 us: shards(): jnp.einsum('rihe,rjhe->hij', grad_heads, split_heads(lax.all_gather(value...]
    another operation x1 -> x0, other arithmetic: 9.38 us -> none  [shards(): jnp.stack([jnp.einsum('hij,rihe->jrhe', dscore_heads, query_heads, prefer...]
  transfers between devices with their start and end apart: 3 -> 0, of which waited for: 3 -> 0; matrix products, arithmetic and copies ran while one was open for 2% -> 0% of each run, Pallas kernels for 0% -> 0%
where the time goes in v2:
time: 106 us
  Pallas kernels  100 us (94%)
  local copies, waits for them, and re-layouts  4.58 us (4%)
    pallas_call x1, Pallas kernels, shards(): pl.pallas_call(functools.partial(kernel, factor), out_shape=jax.ShapeDtyp...  98.4 us
    unnamed x10, local copies, waits for them, and re-layouts  4.58 us
    pallas_call x1, Pallas kernels, shards(): pl.pallas_call(repack, out_shape=(jax.ShapeDtypeStruct(query_proj.shape,...  2.12 us

profile of v2, /device:TPU:8, one launch (start us, length us, event | category | flops | bytes accessed | tf_op | source)
XLA Modules:
  0.0 105.7 jit_solution(15412007199453538204)
XLA Ops:
  0.6 0.0 copy-start.1
  0.6 0.9 copy-done.1
  1.6 0.0 copy-start.2
  1.6 0.9 copy-done.2
  2.5 0.0 copy-start.3
  2.5 0.9 copy-done.3
  3.4 0.0 copy-start.4
  3.4 0.9 copy-done.4
  4.3 98.4 %exchange_and_compute.1.orep = bf16[4,12,64,128]{3,2,1,0:T(8,128)(2,1)S(1)} custom-call(bf16[2,64,768]{2,1,0:T(8,128)(2,1)S(1)} %copy-done.1, bf16[2,64,768]{2,1,0:T(8,128)(2,1)S(1)} %copy-done.2, bf16[2,64,768]{2,1,0:T(8,128)(2,1)S(1)} %copy-done.3, bf16[2,64,768]{2,1,0:T(8,128)(2,1)S(1)} %copy-done.4), custom_call_target="tpu_custom_call" | custom-call | flops 1208000000 | bytes 1600000 | tf_op jit(solution)/shard_map/exchange_and_compute/pallas_call | solution.py:483
  102.7 0.0 copy-start
  102.7 0.9 copy-done
  103.6 2.1 %repack.1 = (bf16[2,64,768]{2,1,0:T(8,128)(2,1)}, bf16[2,64,768]{2,1,0:T(8,128)(2,1)}, bf16[2,64,768]{2,1,0:T(8,128)(2,1)}, bf16[2,64,768]{2,1,0:T(8,128)(2,1)}) custom-call(bf16[4,12,64,128]{3,2,1,0:T(8,128)(2,1)} %copy-done), custom_call_target="tpu_custom_call" | custom-call | tf_op jit(solution)/shard_map/repack/pallas_call | solution.py:501
Async XLA Ops:
  0.6 0.9 copy-start.1
  1.6 0.9 copy-start.2
  2.5 0.9 copy-start.3
  3.4 0.9 copy-start.4
  102.7 0.9 copy-start

commit v3 on v2

--- a/solution.py
+++ b/solution.py
@@ -55,6 +55,7 @@
         )
         self.ring, self.swap, self.core_copy, self.ylo_copy = {}, {}, {}, {}
         self.stat_copy, self.probs_copy, self.edge_copy, self.sums = {}, {}, {}, {}
+        self.arrive, self.leave = {}, {}
 
     @staticmethod
     def scratch(n, cb):
@@ -102,8 +103,13 @@
         mine = self.qg.at[t, self.ours]
         self.swap[t] = self.net.remote(mine, mine, self.net.partner)
 
+    def swap_wait(self, t):
+        copy = self.swap.pop(t, None)
+        if copy is not None:
+            copy.wait_recv()
+
     def s_compute(self, t):
-        self.swap[t].wait_recv()
+        self.swap_wait(t)
         self.part[t] = nt_dot(self.qg[t], self.kv[t])
         other = pl.ds(pl.multiple_of((1 - self.net.core) * self.cb, self.cb), self.cb)
         self.core_copy[t] = self.net.remote(
@@ -159,14 +165,24 @@
         block = self.probs.at[t, self.rows_q]
         self.probs_copy[t] = [
             self.net.remote(block, block, peer)
-            for peer in (self.net.ylo_peer, self.net.far_peer, self.net.core_peer)
+            for peer in (self.net.ylo_peer, self.net.core_peer)
         ]
+
+    def p_forward(self, t):
+        for copy in self.probs_copy[t]:
+            copy.wait_recv()
+        start = self.net.core * self.cb + (1 - self.net.ylo) * self.quarter
+        block = self.probs.at[t, pl.ds(pl.multiple_of(start, self.quarter), self.quarter)]
+        self.probs_copy[t] = [self.net.remote(block, block, self.net.core_peer)]
 
     def out_compute(self, t):
         for copy in self.probs_copy[t]:
             copy.wait_recv()
+        self.swap_wait(1 - t)
         self.rterm[t] = tn_dot(self.probs[t], self.qg[1 - t])
         self.rs_send(t, 1)
+
+    def edge_start(self, t):
         self.eacc[t] = jnp.dot(self.probs[t], self.kv[1 - t], preferred_element_type=F32)
         self.edge[t] = self.eacc[t, self.theirs].astype(BF)
         self.edge_copy[t] = self.net.remote(
@@ -218,16 +234,17 @@
 
 
 class XUnit(Unit):
-    def in_send(self, t):
+    def in_send(self, name, t):
         net = self.net
         lanes = net.lanes(net.x)
-        self.arrive = getattr(self, "arrive", {})
-        for name, array, ref, rows in ((0, t, self.kv, self.own), (1, 2 + t, self.qg, self.ours)):
-            self.arrive[name, t] = [
-                net.remote(net.rep.at[array, NZ + net.xs[k]], ref.at[t, rows, lanes], net.x_peers[k])
-                for k in (2, 1, 3)
-            ]
-            ref[t, rows, lanes] = net.rep[array, NZ + net.x]
+        array, ref, rows = (
+            (t, self.kv, self.own) if name == 0 else (2 + t, self.qg, self.ours)
+        )
+        self.arrive[name, t] = [
+            net.remote(net.rep.at[array, NZ + net.xs[k]], ref.at[t, rows, lanes], net.x_peers[k])
+            for k in (2, 1, 3)
+        ]
+        ref[t, rows, lanes] = net.rep[array, NZ + net.x]
 
     def in_wait(self, name, t):
         for copy in self.arrive[name, t]:
@@ -235,7 +252,6 @@
 
     def out_send(self, index):
         net = self.net
-        self.leave = getattr(self, "leave", {})
         self.leave[index] = [
             net.remote(
                 self.fin.at[index, :, net.lanes(net.xs[k])], net.orep.at[index, NZ + net.x], net.x_peers[k]
@@ -250,30 +266,26 @@
 
 
 class ZUnit(Unit):
-    def in_send(self, t):
+    def in_send(self, name, t):
         net = self.net
         lanes = net.lanes(net.x)
-        self.arrive = getattr(self, "arrive", {})
         slot = net.x * 2 + lax.rem(net.z, 2)
         sub = lax.rem(net.z, 2) * C
-        bases = [net.take(NZ), net.take(NZ)]
+        base = net.take(NZ)
+        array, ref = (t, self.kv) if name == 0 else (2 + t, self.qg)
         for k in (4, 3, 5, 2, 6, 1, 7, 0):
             z_to = lax.rem(net.z + k, NZ)
             x_to = lax.rem(net.z // 2 + z_to, NX)
-            alone = None if k else x_to == net.x
-            for name, array, ref, start in (
-                (0, t, self.kv, x_to * self.cb),
-                (1, 2 + t, self.qg, net.yhi * self.cb),
-            ):
-                dst = ref.at[t, pl.ds(pl.multiple_of(start + sub, C), C), lanes]
-                net.remote(
-                    net.rep.at[array, z_to], dst, net.device(x=x_to, z=z_to),
-                    recv=bases[name] + slot, alone=alone,
-                )
-        for name, ref in ((0, self.kv), (1, self.qg)):
-            self.arrive[name, t] = [
-                (ref.at[t, pl.ds(0, C), pl.ds(0, 128)], bases[name] + k) for k in range(NZ)
-            ]
+            start = (net.yhi if name else x_to) * self.cb + sub
+            net.remote(
+                net.rep.at[array, z_to],
+                ref.at[t, pl.ds(pl.multiple_of(start, C), C), lanes],
+                net.device(x=x_to, z=z_to),
+                recv=base + slot, alone=None if k else x_to == net.x,
+            )
+        self.arrive[name, t] = [
+            (ref.at[t, pl.ds(0, C), pl.ds(0, 128)], base + k) for k in range(NZ)
+        ]
 
     def in_wait(self, name, t):
         for ref, index in self.arrive[name, t]:
@@ -281,7 +293,6 @@
 
     def out_send(self, index):
         net = self.net
-        self.leave = getattr(self, "leave", {})
         pair = lax.rem(net.x - net.z + NZ, NX)
         base = net.take(NZ)
         for k in (2, 1, 3, 0):
@@ -312,7 +323,6 @@
         self.partner = self.device(yhi=1 - self.yhi)
         self.core_peer = self.device(core=1 - self.core)
         self.ylo_peer = self.device(ylo=1 - self.ylo)
-        self.far_peer = self.device(ylo=1 - self.ylo, core=1 - self.core)
         self.sent, self.received, self.started = 0, 0, []
 
     def device(self, **at):
@@ -353,7 +363,8 @@
                 pl.when(jnp.logical_not(alone))(copy.wait_send)
 
 
-def kernel(factor, q_ref, k_ref, v_ref, g_ref, orep, rep, send_sems, recv_sems, *refs):
+def kernel(factor, q_ref, k_ref, v_ref, g_ref, a_out, gq_out, gk_out, gv_out, *refs):
+    staged, results, rep, orep, send_sems, recv_sems, local_sems, *refs = refs
     net = Net(factor, rep, orep, send_sems, recv_sems)
     count = len(refs) // 2
     small = XUnit(
@@ -362,12 +373,18 @@
     )
     big = ZUnit(net, NX, 2 * C, net.x, net.x_peers[1], net.x_peers[3], refs[count:])
 
+    order = ((0, k_ref), (2, q_ref), (1, v_ref), (3, g_ref))
+    fetches = {}
+    for array, ref in order:
+        fetches[array] = pltpu.make_async_copy(ref, staged.at[array], local_sems.at[array])
+        fetches[array].start()
+
     barrier = pltpu.get_barrier_semaphore()
 
     def greet(peer):
         pl.semaphore_signal(barrier, inc=1, device_id=peer, device_id_type=MESH)
 
-    near = net.x_peers[1:] + [small.right, small.left, net.partner, net.core_peer, net.ylo_peer, net.far_peer]
+    near = net.x_peers[1:] + [small.right, small.left, net.partner, net.core_peer, net.ylo_peer]
     pair = lax.rem(net.x - net.z + NZ, NX)
     for k in (2, 1, 3, 0):
         for s in range(2):
@@ -379,19 +396,16 @@
     for peer in near:
         greet(peer)
 
-    for array, ref in ((0, k_ref), (2, q_ref), (1, v_ref), (3, g_ref)):
+    for array, _ in order:
+        fetches[array].wait()
         for m in range(H // 2):
             tile = slice(128 * m, 128 * m + 128)
-            low, high = swap_halves(ref[0, :, tile], ref[1, :, tile])
+            low, high = swap_halves(staged[array, 0, :, tile], staged[array, 1, :, tile])
             rep[array, 2 * m] = low
             rep[array, 2 * m + 1] = high
 
     alone = (lax.rem(net.z // 2 + net.z, NX) == net.x).astype(jnp.int32)
     pl.semaphore_wait(barrier, len(near) + NZ - alone)
-
-    for t in range(2):
-        small.in_send(t)
-        big.in_send(t)
 
     def ring_start(unit, t):
         unit.in_wait(0, t)
@@ -401,76 +415,106 @@
         unit.in_wait(1, t)
         unit.swap_start(t)
 
+    small.in_send(0, 0)
+    big.in_send(0, 0)
     ring_start(small, 0)
+    big.in_send(1, 0)
+    small.in_send(1, 0)
+    small.in_send(0, 1)
+    small.ring_step(0, 1)
+    ring_start(big, 0)
+    ring_start(small, 1)
+    small.ring_step(0, 2)
+    small.in_send(1, 1)
+    swap_start(big, 0)
+    big.ring_step(0, 1)
+    small.ring_step(1, 1)
+    big.in_send(0, 1)
+    swap_start(small, 1)
     swap_start(small, 0)
-    ring_start(small, 1)
-    swap_start(small, 1)
-    ring_start(big, 0)
-    swap_start(big, 0)
-    small.ring_step(0, 1)
-    small.ring_step(1, 1)
-    small.ring_step(0, 2)
-    ring_start(big, 1)
-    swap_start(big, 1)
-    big.ring_step(0, 1)
-    small.ring_step(1, 2)
     small.ring_step(0, 3)
     big.ring_step(0, 2)
+    big.in_send(1, 1)
     big.s_compute(0)
+    small.ring_step(1, 2)
+    small.ring_step(0, 4)
+    big.s_core(0)
+    ring_start(big, 1)
+    small.s_compute(0)
+    small.s_core(0)
     small.ring_step(1, 3)
+    swap_start(big, 1)
+    small.s_reduce(0)
+    small.ring_step(1, 4)
+    small.s_compute(1)
     big.ring_step(1, 1)
-    big.s_core(0)
-    small.ring_step(0, 4)
-    small.s_compute(0)
-    small.ring_step(1, 4)
-    small.s_core(0)
+    big.s_reduce(0)
+    small.s_core(1)
+    small.p_compute(0)
     big.ring_step(1, 2)
     big.s_compute(1)
-    small.s_compute(1)
+    big.p_compute(0)
+    small.s_reduce(1)
     big.s_core(1)
-    small.s_core(1)
-    big.s_reduce(0)
-    small.s_reduce(0)
-    big.p_compute(0)
-    small.p_compute(0)
+    small.p_forward(0)
+    small.out_compute(0)
+    small.p_compute(1)
+    big.p_forward(0)
+    small.rs_send(0, 2)
     big.s_reduce(1)
-    small.s_reduce(1)
     big.out_compute(0)
-    small.out_compute(0)
-    big.p_compute(1)
-    small.p_compute(1)
-    big.rs_send(0, 2)
-    small.rs_send(0, 2)
-    big.out_compute(1)
+    big.edge_start(0)
+    small.p_forward(1)
     small.out_compute(1)
     small.rs_send(0, 3)
+    big.rs_send(0, 2)
+    big.p_compute(1)
+    small.rs_send(1, 2)
     big.edge_end(0)
+    big.p_forward(1)
+    small.rs_send(1, 3)
+    big.out_compute(1)
+    big.edge_start(1)
+    big.rs_end(0)
+    small.rs_send(1, 4)
+    big.rs_send(1, 2)
+    small.edge_start(1)
+    small.rs_send(0, 4)
+    big.edge_end(1)
+    small.rs_end(1)
+    small.edge_start(0)
+    small.edge_end(1)
+    small.rs_end(0)
+    big.rs_end(1)
     small.edge_end(0)
-    big.rs_end(0)
-    small.rs_send(1, 2)
-    big.rs_send(1, 2)
-    small.rs_send(0, 4)
-    small.rs_send(1, 3)
-    big.edge_end(1)
-    small.edge_end(1)
-    big.rs_end(1)
-    small.rs_end(0)
-    small.rs_send(1, 4)
-    small.rs_end(1)
-
-    for unit in (big, small):
-        for index in range(4):
-            unit.out_wait(index)
-    net.finish()
-
-
-def repack(orep, *outs):
-    for array, ref in enumerate(outs):
+
+    stores = []
+    for index, ref in ((0, a_out), (1, gq_out), (3, gv_out), (2, gk_out)):
+        big.out_wait(index)
+        small.out_wait(index)
         for m in range(H // 2):
             tile = slice(128 * m, 128 * m + 128)
-            first, second = swap_halves(orep[array, 2 * m], orep[array, 2 * m + 1])
-            ref[0, :, tile] = first
-            ref[1, :, tile] = second
+            first, second = swap_halves(orep[index, 2 * m], orep[index, 2 * m + 1])
+            results[index, 0, :, tile] = first
+            results[index, 1, :, tile] = second
+        stores.append(pltpu.make_async_copy(results.at[index], ref, local_sems.at[4 + index]))
+        stores[-1].start()
+    net.finish()
+    for copy in stores:
+        copy.wait()
+
+
+def hand_over(*refs):
+    sources, targets, held, sems = refs[:4], refs[4:8], refs[8], refs[9]
+    reads = [pltpu.make_async_copy(sources[i], held.at[i], sems.at[i]) for i in range(4)]
+    writes = [pltpu.make_async_copy(held.at[i], targets[i], sems.at[4 + i]) for i in range(4)]
+    for copy in reads:
+        copy.start()
+    for read, write in zip(reads, writes):
+        read.wait()
+        write.start()
+    for copy in writes:
+        copy.wait()
 
 
 COPIES = 180
@@ -479,32 +523,38 @@
 def shards(query_proj, key_proj, value_proj, grad_output):
     row_count = query_proj.shape[0] * lax.axis_size("row")
     factor = 1.0 / math.sqrt(D // H * row_count)
-    vmem = pl.BlockSpec(memory_space=pltpu.VMEM)
-    blocks = pl.pallas_call(
+    anywhere = pl.BlockSpec(memory_space=pl.ANY)
+    shape = query_proj.shape
+    results = pl.pallas_call(
         functools.partial(kernel, factor),
-        out_shape=jax.ShapeDtypeStruct((4, H, C, 128), BF),
-        in_specs=[vmem] * 4,
-        out_specs=vmem,
+        out_shape=(jax.ShapeDtypeStruct(shape, BF),) * 4,
+        in_specs=[anywhere] * 4,
+        out_specs=(anywhere,) * 4,
         scratch_shapes=[
+            pltpu.VMEM((4, *shape), BF),
+            pltpu.VMEM((4, *shape), BF),
+            pltpu.VMEM((4, H, C, 128), BF),
             pltpu.VMEM((4, H, C, 128), BF),
             pltpu.SemaphoreType.DMA((COPIES,)),
             pltpu.SemaphoreType.DMA((COPIES,)),
+            pltpu.SemaphoreType.DMA((8,)),
             *Unit.scratch(NZ, C),
             *Unit.scratch(NX, 2 * C),
         ],
         compiler_params=pltpu.CompilerParams(
-            collective_id=0, has_side_effects=True, vmem_limit_bytes=48 * 2**20
+            collective_id=0, has_side_effects=True, vmem_limit_bytes=60 * 2**20
         ),
         cost_estimate=pl.CostEstimate(flops=1_208_000_000, bytes_accessed=1_600_000, transcendentals=50_000),
         name="exchange_and_compute",
     )(query_proj, key_proj, value_proj, grad_output)
     return pl.pallas_call(
-        repack,
-        out_shape=(jax.ShapeDtypeStruct(query_proj.shape, BF),) * 4,
-        in_specs=[vmem],
-        out_specs=(vmem,) * 4,
-        name="repack",
-    )(blocks)
+        hand_over,
+        out_shape=(jax.ShapeDtypeStruct(shape, BF),) * 4,
+        in_specs=[anywhere] * 4,
+        out_specs=(anywhere,) * 4,
+        scratch_shapes=[pltpu.VMEM((4, *shape), BF), pltpu.SemaphoreType.DMA((8,))],
+        name="hand_over",
+    )(*results)
 
 
 def solution(mesh):

time: 106 us -> 86.7 us (0.82)
  Pallas kernels: 100 us -> 85.9 us
  local copies, waits for them, and re-layouts: 4.58 us -> 0 us
    pallas_call x2, Pallas kernels: 100 us -> 85.9 us  [the longest x1 84 us: shards(): pl.pallas_call(functools.partial(kernel, factor), out_shape=(jax.ShapeDty...]
    unnamed x10 -> x0, local copies, waits for them, and re-layouts: 4.58 us -> none
where the time goes in v3:
time: 86.7 us; the launch traced here: 86.6 us
  Pallas kernels  85.9 us (99%)
    pallas_call x1, Pallas kernels, shards(): pl.pallas_call(functools.partial(kernel, factor), out_shape=(jax.ShapeDty...  84 us
    pallas_call x1, Pallas kernels, shards(): pl.pallas_call(hand_over, out_shape=(jax.ShapeDtypeStruct(shape, BF),) *...  1.97 us

profile of v3, /device:TPU:8, one launch (start us, length us, event | category | flops | bytes accessed | tf_op | source)
XLA Modules:
  0.0 86.6 jit_solution(310068032066385572)
XLA Ops:
  0.6 84.0 %exchange_and_compute.1 = (bf16[2,64,768]{2,1,0:T(8,128)(2,1)}, bf16[2,64,768]{2,1,0:T(8,128)(2,1)}, bf16[2,64,768]{2,1,0:T(8,128)(2,1)}, bf16[2,64,768]{2,1,0:T(8,128)(2,1)}) custom-call(bf16[2,64,768]{2,1,0:T(8,128)(2,1)} %q_ref.1, bf16[2,64,768]{2,1,0:T(8,128)(2,1)} %k_ref.1, bf16[2,64,768]{2,1,0:T(8,128)(2,1)} %v_ref.1, bf16[2,64,768]{2,1,0:T(8,128)(2,1)} %g_ref.1), custom_call_target="tpu_custom_call" | custom-call | flops 1208000000 | bytes 1600000 | tf_op jit(solution)/shard_map/exchange_and_compute/pallas_call | solution.py:528
  84.6 2.0 %hand_over.1 = (bf16[2,64,768]{2,1,0:T(8,128)(2,1)}, bf16[2,64,768]{2,1,0:T(8,128)(2,1)}, bf16[2,64,768]{2,1,0:T(8,128)(2,1)}, bf16[2,64,768]{2,1,0:T(8,128)(2,1)}) custom-call(bf16[2,64,768]{2,1,0:T(8,128)(2,1)} %get-tuple-element.8.refs_0_, bf16[2,64,768]{2,1,0:T(8,128)(2,1)} %get-tuple-element.9.refs_1_, bf16[2,64,768]{2,1,0:T(8,128)(2,1)} %get-tuple-element.10.refs_2_, ...), custom_call_target="tpu_custom_call" | custom-call | tf_op jit(solution)/shard_map/hand_over/pallas_call | solution.py:550

commit v4 on v3

--- a/solution.py
+++ b/solution.py
@@ -15,6 +15,7 @@
 C = 64
 W = 512
 J = 512
+POOL_MAX, POOL_STEP = 2**20, 2**14
 MESH = pl.DeviceIdType.MESH
 BF = jnp.bfloat16
 F32 = jnp.float32
@@ -38,8 +39,9 @@
 
 
 class Unit:
-    def __init__(self, net, n, cb, me, right, left, refs):
+    def __init__(self, net, n, cb, me, right, left, whole, refs):
         self.net, self.n, self.cb, self.me = net, n, cb, me
+        self.whole = whole
         self.right, self.left = right, left
         (
             self.kv, self.qg, self.part, self.core_in, self.half, self.ylo_in, self.stat, self.stat_in,
@@ -49,27 +51,29 @@
         self.ours = pl.ds(pl.multiple_of(net.yhi * cb, cb), cb)
         self.theirs = pl.ds(pl.multiple_of((1 - net.yhi) * cb, cb), cb)
         self.own = pl.ds(self.block(0), cb)
-        self.quarter = cb // 2
+        self.quarter = cb if whole else cb // 2
+        self.part_of_half = 0 if whole else net.ylo
         self.rows_q = pl.ds(
-            pl.multiple_of(net.core * cb + net.ylo * self.quarter, self.quarter), self.quarter
+            pl.multiple_of(net.core * cb + self.part_of_half * self.quarter, self.quarter), self.quarter
         )
         self.ring, self.swap, self.core_copy, self.ylo_copy = {}, {}, {}, {}
         self.stat_copy, self.probs_copy, self.edge_copy, self.sums = {}, {}, {}, {}
         self.arrive, self.leave = {}, {}
 
     @staticmethod
-    def scratch(n, cb):
+    def scratch(n, cb, whole):
+        quarter = cb if whole else cb // 2
         return [
             pltpu.VMEM((2, J, W), BF),
             pltpu.VMEM((2, 2 * cb, W), BF),
             pltpu.VMEM((2, 2 * cb, J), F32),
             pltpu.VMEM((2, cb, J), F32),
             pltpu.VMEM((2, cb, J), F32),
-            pltpu.VMEM((2, cb // 2, J), F32),
-            pltpu.VMEM((2, cb // 2, 128), F32),
-            pltpu.VMEM((2, cb // 2, 128), F32),
+            pltpu.VMEM((2, quarter, J), F32),
+            pltpu.VMEM((2, 8, 128), F32),
+            pltpu.VMEM((2, 8, 128), F32),
             pltpu.VMEM((2, 2 * cb, J), BF),
-            pltpu.VMEM((2, cb // 2, J), F32),
+            pltpu.VMEM((2, quarter, J), F32),
             pltpu.VMEM((2, 2 * cb, W), F32),
             pltpu.VMEM((2, cb, W), BF),
             pltpu.VMEM((2, cb, W), BF),
@@ -88,14 +92,12 @@
         left_block = self.block(step - 1)
         there = self.kv.at[t, pl.ds(self.block(1 - step), size)]
         back = self.kv.at[t, pl.ds(left_block if full else left_block + self.cb // 2, size)]
-        self.ring[t, step] = (
-            self.net.remote(there, there, self.right),
-            self.net.remote(back, back, self.left),
-        )
+        recv = self.net.remote(there, there, self.right)
+        self.ring[t, step] = self.net.remote(back, back, self.left, recv=recv)
 
     def ring_step(self, t, step):
-        for copy in self.ring[t, step]:
-            copy.wait_recv()
+        size = 2 * self.cb if step < self.n // 2 else self.cb
+        self.net.wait_recv(self.kv.at[t, pl.ds(0, size)], self.ring[t, step])
         if step < self.n // 2:
             self.ring_send(t, step + 1)
 
@@ -104,9 +106,9 @@
         self.swap[t] = self.net.remote(mine, mine, self.net.partner)
 
     def swap_wait(self, t):
-        copy = self.swap.pop(t, None)
-        if copy is not None:
-            copy.wait_recv()
+        recv = self.swap.pop(t, None)
+        if recv is not None:
+            self.net.wait_recv(self.qg.at[t, self.theirs], recv)
 
     def s_compute(self, t):
         self.swap_wait(t)
@@ -117,67 +119,72 @@
         )
 
     def s_core(self, t):
-        self.core_copy[t].wait_recv()
+        self.net.wait_recv(self.core_in.at[t], self.core_copy[t])
         rows = pl.ds(pl.multiple_of(self.net.core * self.cb, self.cb), self.cb)
         self.half[t] = self.part[t, rows] + self.core_in[t]
-        other = pl.ds(
-            pl.multiple_of((1 - self.net.ylo) * self.quarter, self.quarter), self.quarter
-        )
+        start = 0 if self.whole else (1 - self.net.ylo) * self.quarter
+        other = pl.ds(pl.multiple_of(start, self.quarter), self.quarter)
         self.ylo_copy[t] = self.net.remote(
             self.half.at[t, other], self.ylo_in.at[t], self.net.ylo_peer
         )
 
     def s_reduce(self, t):
-        self.ylo_copy[t].wait_recv()
-        rows = pl.ds(pl.multiple_of(self.net.ylo * self.quarter, self.quarter), self.quarter)
+        self.net.wait_recv(self.ylo_in.at[t], self.ylo_copy[t])
+        rows = pl.ds(pl.multiple_of(self.part_of_half * self.quarter, self.quarter), self.quarter)
         total = self.half[t, rows] + self.ylo_in[t]
         if t == 0:
             score = total * self.net.factor
             top = jnp.max(score, axis=1, keepdims=True)
             weight = jnp.exp(score - top)
             self.mine[0] = weight
-            lane = lax.broadcasted_iota(jnp.int32, (self.quarter, 128), 1)
-            self.stat[0] = jnp.where(lane == 0, top, jnp.sum(weight, axis=1, keepdims=True))
+            self.stat[0] = self.to_rows(top, jnp.sum(weight, axis=1, keepdims=True))
         else:
             self.mine[1] = total
             dot = jnp.sum(self.mine[0] * total, axis=1, keepdims=True)
-            self.stat[1] = jnp.broadcast_to(dot, (self.quarter, 128))
+            self.stat[1] = self.to_rows(dot, dot)
         self.stat_copy[t] = self.net.remote(
             self.stat.at[t], self.stat_in.at[t], self.net.partner
         )
 
+    def to_rows(self, first, second):
+        lane = lax.broadcasted_iota(jnp.int32, (self.quarter, 128), 1)
+        wide = jnp.where(lane == 0, first, second)
+        wide = jnp.concatenate([wide] * (128 // self.quarter), axis=0)
+        return wide.T[:8]
+
+    def to_columns(self, rows):
+        wide = jnp.concatenate([rows] * 16, axis=0).T[: self.quarter]
+        return wide[:, 0:1], wide[:, 1:2]
+
     def p_compute(self, t):
-        self.stat_copy[t].wait_recv()
-        here, there = self.stat[t], self.stat_in[t]
+        self.net.wait_recv(self.stat_in.at[t], self.stat_copy[t])
+        top_a, total_a = self.to_columns(self.stat[t])
+        top_b, total_b = self.to_columns(self.stat_in[t])
         if t == 0:
-            top_a, top_b = here[:, 0:1], there[:, 0:1]
             top = jnp.maximum(top_a, top_b)
             scale_a, scale_b = jnp.exp(top_a - top), jnp.exp(top_b - top)
-            total = here[:, 1:2] * scale_a + there[:, 1:2] * scale_b
+            total = total_a * scale_a + total_b * scale_b
             weights = self.mine[0] * (scale_a / total)
             self.mine[0] = weights
             self.probs[0, self.rows_q] = weights.astype(BF)
         else:
-            row_dot = here[:, 0:1] + there[:, 0:1]
+            row_dot = top_a + top_b
             self.probs[1, self.rows_q] = (
                 self.net.factor * self.mine[0] * (self.mine[1] - row_dot)
             ).astype(BF)
         block = self.probs.at[t, self.rows_q]
-        self.probs_copy[t] = [
-            self.net.remote(block, block, peer)
-            for peer in (self.net.ylo_peer, self.net.core_peer)
-        ]
+        recv = None if self.whole else self.net.remote(block, block, self.net.ylo_peer)
+        self.probs_copy[t] = self.net.remote(block, block, self.net.core_peer, recv=recv)
 
     def p_forward(self, t):
-        for copy in self.probs_copy[t]:
-            copy.wait_recv()
+        arrived = self.probs.at[t, pl.ds(0, 2 * self.quarter)]
+        self.net.wait_recv(arrived, self.probs_copy[t])
         start = self.net.core * self.cb + (1 - self.net.ylo) * self.quarter
         block = self.probs.at[t, pl.ds(pl.multiple_of(start, self.quarter), self.quarter)]
-        self.probs_copy[t] = [self.net.remote(block, block, self.net.core_peer)]
+        self.probs_copy[t] = self.net.remote(block, block, self.net.core_peer)
 
     def out_compute(self, t):
-        for copy in self.probs_copy[t]:
-            copy.wait_recv()
+        self.net.wait_recv(self.probs.at[t, pl.ds(0, self.quarter)], self.probs_copy[t])
         self.swap_wait(1 - t)
         self.rterm[t] = tn_dot(self.probs[t], self.qg[1 - t])
         self.rs_send(t, 1)
@@ -191,16 +198,18 @@
 
     def rs_send(self, t, step):
         cb, half = self.cb, self.cb // 2
+        if step > 1:
+            self.rs_wait(t, step - 1)
+        recv = None
         for way, peer in ((0, self.right), (1, self.left)):
             start = self.block((self.n // 2 + 1 - step) * (1 if way == 0 else -1))
             first, rest = slice(half * way, half * way + half), slice(half - half * way, cb - half * way)
             send = self.rsend.at[t, way, step - 1]
-            recv = self.rrecv.at[t, way, step - 1]
+            into = self.rrecv.at[t, way, step - 1]
             if step == 1:
                 send[first] = self.rterm[t, pl.ds(start + half * way, half)].astype(BF)
-                send, recv = (ref.at[pl.ds(half * way, half)] for ref in (send, recv))
+                send, into = (ref.at[pl.ds(half * way, half)] for ref in (send, into))
             else:
-                self.sums[t, step - 1][way].wait_recv()
                 arrived = self.rrecv.at[t, way, step - 2]
                 if step == 2:
                     send[first] = (
@@ -211,12 +220,16 @@
                     send[...] = (
                         self.rterm[t, pl.ds(start, cb)] + arrived[...].astype(F32)
                     ).astype(BF)
-            self.sums.setdefault((t, step), []).append(self.net.remote(send, recv, peer))
+            recv = self.net.remote(send, into, peer, recv=recv)
+        self.sums[t, step] = recv
+
+    def rs_wait(self, t, step):
+        size = self.cb // 2 if step == 1 else self.cb
+        self.net.wait_recv(self.rrecv.at[t, :, step - 1, pl.ds(0, size)], self.sums[t, step])
 
     def rs_end(self, t):
         last = self.n // 2
-        for copy in self.sums[t, last]:
-            copy.wait_recv()
+        self.rs_wait(t, last)
         index = (GRAD_VALUE, GRAD_KEY)[t]
         self.fin[index] = (
             self.rterm[t, self.own]
@@ -225,7 +238,7 @@
         self.out_send(index)
 
     def edge_end(self, t):
-        self.edge_copy[t].wait_recv()
+        self.net.wait_recv(self.edge_in.at[t], self.edge_copy[t])
         index = (ATTENDED, GRAD_QUERY)[t]
         self.fin[index] = (
             self.eacc[t, self.ours] + self.edge_in[t].astype(F32)
@@ -240,38 +253,39 @@
         array, ref, rows = (
             (t, self.kv, self.own) if name == 0 else (2 + t, self.qg, self.ours)
         )
-        self.arrive[name, t] = [
-            net.remote(net.rep.at[array, NZ + net.xs[k]], ref.at[t, rows, lanes], net.x_peers[k])
-            for k in (2, 1, 3)
-        ]
+        recv = net.take()
+        for k in (2, 1, 3):
+            net.remote(
+                net.rep.at[array, NZ + net.xs[k]], ref.at[t, rows, lanes], net.x_peers[k], recv=recv
+            )
+        self.arrive[name, t] = recv
         ref[t, rows, lanes] = net.rep[array, NZ + net.x]
 
     def in_wait(self, name, t):
-        for copy in self.arrive[name, t]:
-            copy.wait_recv()
+        ref, rows = (self.kv, self.own) if name == 0 else (self.qg, self.ours)
+        self.net.wait_recv(ref.at[t, rows, pl.ds(0, 3 * 128)], self.arrive[name, t])
 
     def out_send(self, index):
         net = self.net
-        self.leave[index] = [
+        recv = net.take()
+        for k in (2, 1, 3):
             net.remote(
-                self.fin.at[index, :, net.lanes(net.xs[k])], net.orep.at[index, NZ + net.x], net.x_peers[k]
+                self.fin.at[index, :, net.lanes(net.xs[k])], net.orep.at[index, NZ + net.x],
+                net.x_peers[k], recv=recv,
             )
-            for k in (2, 1, 3)
-        ]
+        self.leave[index] = recv
         net.orep[index, NZ + net.x] = self.fin[index, :, net.lanes(net.x)]
 
     def out_wait(self, index):
-        for copy in self.leave[index]:
-            copy.wait_recv()
+        self.net.wait_recv(self.net.orep.at[index, pl.ds(NZ, 3)], self.leave[index])
 
 
 class ZUnit(Unit):
     def in_send(self, name, t):
         net = self.net
         lanes = net.lanes(net.x)
-        slot = net.x * 2 + lax.rem(net.z, 2)
         sub = lax.rem(net.z, 2) * C
-        base = net.take(NZ)
+        recv = net.take()
         array, ref = (t, self.kv) if name == 0 else (2 + t, self.qg)
         for k in (4, 3, 5, 2, 6, 1, 7, 0):
             z_to = lax.rem(net.z + k, NZ)
@@ -281,20 +295,18 @@
                 net.rep.at[array, z_to],
                 ref.at[t, pl.ds(pl.multiple_of(start, C), C), lanes],
                 net.device(x=x_to, z=z_to),
-                recv=base + slot, alone=None if k else x_to == net.x,
+                recv=recv, alone=None if k else x_to == net.x, key="in",
             )
-        self.arrive[name, t] = [
-            (ref.at[t, pl.ds(0, C), pl.ds(0, 128)], base + k) for k in range(NZ)
-        ]
+        self.arrive[name, t] = recv
 
     def in_wait(self, name, t):
-        for ref, index in self.arrive[name, t]:
-            self.net.wait_recv(ref, index)
+        block = self.kv.at[t, self.own] if name == 0 else self.qg.at[t, self.ours]
+        self.net.wait_recv(block, self.arrive[name, t])
 
     def out_send(self, index):
         net = self.net
         pair = lax.rem(net.x - net.z + NZ, NX)
-        base = net.take(NZ)
+        recv = net.take()
         for k in (2, 1, 3, 0):
             for s in range(2):
                 z_to = pair * 2 + s
@@ -302,13 +314,12 @@
                     self.fin.at[index, pl.ds(s * C, C), net.lanes(net.xs[k])],
                     net.orep.at[index, net.z],
                     net.device(x=net.xs[k], z=z_to),
-                    recv=base + net.z, alone=None if k else z_to == net.z,
+                    recv=recv, alone=None if k else z_to == net.z, key=("out", s),
                 )
-        self.leave[index] = [(net.orep.at[index, k], base + k) for k in range(NZ)]
+        self.leave[index] = recv
 
     def out_wait(self, index):
-        for ref, slot in self.leave[index]:
-            self.net.wait_recv(ref, slot)
+        self.net.wait_recv(self.net.orep.at[index, pl.ds(0, NZ)], self.leave[index])
 
 
 class Net:
@@ -323,7 +334,7 @@
         self.partner = self.device(yhi=1 - self.yhi)
         self.core_peer = self.device(core=1 - self.core)
         self.ylo_peer = self.device(ylo=1 - self.ylo)
-        self.sent, self.received, self.started = 0, 0, []
+        self.received, self.groups, self.pools = 0, [], {}
 
     def device(self, **at):
         ylo, x, core, z, yhi = (at.get(k, getattr(self, k)) for k in ("ylo", "x", "core", "z", "yhi"))
@@ -332,31 +343,48 @@
     def lanes(self, x):
         return pl.ds(pl.multiple_of(x * 128, 128), 128)
 
-    def take(self, n):
-        self.received += n
-        return self.received - n
-
-    def remote(self, src, dst, peer, recv=None, alone=None):
-        recv = self.take(1) if recv is None else recv
-        send = self.send_sems.at[self.sent]
-        self.sent += 1
+    def take(self):
+        self.received += 1
+        return self.received - 1
+
+    def remote(self, src, dst, peer, recv=None, alone=None, key=None):
+        recv = self.take() if recv is None else recv
+        size = math.prod(src.shape) * src.dtype.itemsize
+        if alone is None:
+            name = "small" if size < POOL_STEP else "pool"
+            group = self.pools.get(name)
+            if group is None or group[1] + size > POOL_MAX:
+                group = self.new_group(None)
+                self.pools[name] = group
+        else:
+            group = self.pools.get(key) or self.new_group(alone)
+            self.pools[key] = group
+        group[1] += size
         copy = pltpu.make_async_remote_copy(
-            src_ref=src, dst_ref=dst, send_sem=send, recv_sem=self.recv_sems.at[recv],
-            device_id=peer, device_id_type=MESH,
+            src_ref=src, dst_ref=dst, send_sem=self.send_sems.at[group[0]],
+            recv_sem=self.recv_sems.at[recv], device_id=peer, device_id_type=MESH,
         )
         if alone is None:
             copy.start()
         else:
             pl.when(jnp.logical_not(alone))(copy.start)
             pl.when(alone)(pltpu.make_async_copy(src, dst, self.recv_sems.at[recv]).start)
-        self.started.append((copy, alone))
-        return copy
+        return recv
+
+    def new_group(self, alone):
+        self.groups.append([len(self.groups), 0, alone])
+        return self.groups[-1]
 
     def wait_recv(self, ref, index):
         pltpu.make_async_copy(ref, ref, self.recv_sems.at[index]).wait()
 
-    def finish(self):
-        for copy, alone in self.started:
+    def finish(self, ref):
+        for index, size, alone in self.groups:
+            view = ref.at[pl.ds(0, size // 2048)]
+            copy = pltpu.make_async_remote_copy(
+                src_ref=view, dst_ref=view, send_sem=self.send_sems.at[index],
+                recv_sem=self.recv_sems.at[0], device_id=self.partner, device_id_type=MESH,
+            )
             if alone is None:
                 copy.wait_send()
             else:
@@ -369,9 +397,9 @@
     count = len(refs) // 2
     small = XUnit(
         net, NZ, C, net.z,
-        net.device(z=lax.rem(net.z + 1, NZ)), net.device(z=lax.rem(net.z + NZ - 1, NZ)), refs[:count],
+        net.device(z=lax.rem(net.z + 1, NZ)), net.device(z=lax.rem(net.z + NZ - 1, NZ)), True, refs[:count],
     )
-    big = ZUnit(net, NX, 2 * C, net.x, net.x_peers[1], net.x_peers[3], refs[count:])
+    big = ZUnit(net, NX, 2 * C, net.x, net.x_peers[1], net.x_peers[3], False, refs[count:])
 
     order = ((0, k_ref), (2, q_ref), (1, v_ref), (3, g_ref))
     fetches = {}
@@ -415,78 +443,76 @@
         unit.in_wait(1, t)
         unit.swap_start(t)
 
+    big.in_send(0, 0)
+    small.in_send(1, 0)
     small.in_send(0, 0)
-    big.in_send(0, 0)
+    big.in_send(1, 0)
+    small.in_send(0, 1)
     ring_start(small, 0)
-    big.in_send(1, 0)
-    small.in_send(1, 0)
-    small.in_send(0, 1)
-    small.ring_step(0, 1)
     ring_start(big, 0)
     ring_start(small, 1)
-    small.ring_step(0, 2)
+    small.ring_step(0, 1)
     small.in_send(1, 1)
+    big.in_send(0, 1)
     swap_start(big, 0)
     big.ring_step(0, 1)
+    swap_start(small, 0)
+    swap_start(small, 1)
+    small.ring_step(0, 2)
     small.ring_step(1, 1)
-    big.in_send(0, 1)
-    swap_start(small, 1)
-    swap_start(small, 0)
+    big.ring_step(0, 2)
+    big.s_compute(0)
     small.ring_step(0, 3)
-    big.ring_step(0, 2)
     big.in_send(1, 1)
-    big.s_compute(0)
+    big.s_core(0)
+    small.ring_step(0, 4)
+    small.s_compute(0)
+    ring_start(big, 1)
     small.ring_step(1, 2)
-    small.ring_step(0, 4)
-    big.s_core(0)
-    ring_start(big, 1)
-    small.s_compute(0)
     small.s_core(0)
+    big.s_reduce(0)
+    swap_start(big, 1)
     small.ring_step(1, 3)
-    swap_start(big, 1)
+    big.ring_step(1, 1)
     small.s_reduce(0)
     small.ring_step(1, 4)
     small.s_compute(1)
-    big.ring_step(1, 1)
-    big.s_reduce(0)
+    big.p_compute(0)
+    big.ring_step(1, 2)
     small.s_core(1)
     small.p_compute(0)
-    big.ring_step(1, 2)
     big.s_compute(1)
-    big.p_compute(0)
+    small.out_compute(0)
+    big.p_forward(0)
+    big.s_core(1)
+    big.out_compute(0)
+    small.rs_send(0, 2)
     small.s_reduce(1)
-    big.s_core(1)
-    small.p_forward(0)
-    small.out_compute(0)
+    big.rs_send(0, 2)
+    small.rs_send(0, 3)
+    big.s_reduce(1)
     small.p_compute(1)
-    big.p_forward(0)
-    small.rs_send(0, 2)
-    big.s_reduce(1)
-    big.out_compute(0)
+    small.out_compute(1)
+    big.p_compute(1)
+    small.rs_send(0, 4)
     big.edge_start(0)
-    small.p_forward(1)
-    small.out_compute(1)
-    small.rs_send(0, 3)
-    big.rs_send(0, 2)
-    big.p_compute(1)
     small.rs_send(1, 2)
-    big.edge_end(0)
+    big.rs_end(0)
     big.p_forward(1)
     small.rs_send(1, 3)
     big.out_compute(1)
     big.edge_start(1)
-    big.rs_end(0)
+    small.edge_start(0)
+    big.edge_end(0)
+    big.rs_send(1, 2)
     small.rs_send(1, 4)
-    big.rs_send(1, 2)
     small.edge_start(1)
-    small.rs_send(0, 4)
     big.edge_end(1)
+    big.rs_end(1)
     small.rs_end(1)
-    small.edge_start(0)
     small.edge_end(1)
+    small.edge_end(0)
     small.rs_end(0)
-    big.rs_end(1)
-    small.edge_end(0)
 
     stores = []
     for index, ref in ((0, a_out), (1, gq_out), (3, gv_out), (2, gk_out)):
@@ -499,7 +525,7 @@
             results[index, 1, :, tile] = second
         stores.append(pltpu.make_async_copy(results.at[index], ref, local_sems.at[4 + index]))
         stores[-1].start()
-    net.finish()
+    net.finish(small.rterm.at[0])
     for copy in stores:
         copy.wait()
 
@@ -517,7 +543,7 @@
         copy.wait()
 
 
-COPIES = 180
+SENDS, RECEIVES = 12, 66
 
 
 def shards(query_proj, key_proj, value_proj, grad_output):
@@ -535,11 +561,11 @@
             pltpu.VMEM((4, *shape), BF),
             pltpu.VMEM((4, H, C, 128), BF),
             pltpu.VMEM((4, H, C, 128), BF),
-            pltpu.SemaphoreType.DMA((COPIES,)),
-            pltpu.SemaphoreType.DMA((COPIES,)),
+            pltpu.SemaphoreType.DMA((SENDS,)),
+            pltpu.SemaphoreType.DMA((RECEIVES,)),
             pltpu.SemaphoreType.DMA((8,)),
-            *Unit.scratch(NZ, C),
-            *Unit.scratch(NX, 2 * C),
+            *Unit.scratch(NZ, C, True),
+            *Unit.scratch(NX, 2 * C, False),
         ],
         compiler_params=pltpu.CompilerParams(
             collective_id=0, has_side_effects=True, vmem_limit_bytes=60 * 2**20

time: 86.7 us -> 84.4 us (0.973); the launches traced: 86.6 us -> 83.4 us
  Pallas kernels: 85.9 us -> 82.7 us
    pallas_call x1, Pallas kernels: 84 us -> 80.8 us  [shards(): pl.pallas_call(functools.partial(kernel, factor), out_shape=(jax.ShapeDty...]
where the time goes in v4:
time: 84.4 us; the launch traced here: 83.4 us
  Pallas kernels  82.7 us (98%)
    pallas_call x1, Pallas kernels, shards(): pl.pallas_call(functools.partial(kernel, factor), out_shape=(jax.ShapeDty...  80.8 us
    pallas_call x1, Pallas kernels, shards(): pl.pallas_call(hand_over, out_shape=(jax.ShapeDtypeStruct(shape, BF),) *...  1.97 us

profile of v4, /device:TPU:8, one launch (start us, length us, event | category | flops | bytes accessed | tf_op | source)
XLA Modules:
  0.0 83.4 jit_solution(2530189576619465941)
XLA Ops:
  0.6 80.8 %exchange_and_compute.1 = (bf16[2,64,768]{2,1,0:T(8,128)(2,1)}, bf16[2,64,768]{2,1,0:T(8,128)(2,1)}, bf16[2,64,768]{2,1,0:T(8,128)(2,1)}, bf16[2,64,768]{2,1,0:T(8,128)(2,1)}) custom-call(bf16[2,64,768]{2,1,0:T(8,128)(2,1)} %q_ref.1, bf16[2,64,768]{2,1,0:T(8,128)(2,1)} %k_ref.1, bf16[2,64,768]{2,1,0:T(8,128)(2,1)} %v_ref.1, bf16[2,64,768]{2,1,0:T(8,128)(2,1)} %g_ref.1), custom_call_target="tpu_custom_call" | custom-call | flops 1208000000 | bytes 1600000 | tf_op jit(solution)/shard_map/exchange_and_compute/pallas_call | solution.py:554
  81.4 2.0 %hand_over.1 = (bf16[2,64,768]{2,1,0:T(8,128)(2,1)}, bf16[2,64,768]{2,1,0:T(8,128)(2,1)}, bf16[2,64,768]{2,1,0:T(8,128)(2,1)}, bf16[2,64,768]{2,1,0:T(8,128)(2,1)}) custom-call(bf16[2,64,768]{2,1,0:T(8,128)(2,1)} %get-tuple-element.8.refs_0_, bf16[2,64,768]{2,1,0:T(8,128)(2,1)} %get-tuple-element.9.refs_1_, bf16[2,64,768]{2,1,0:T(8,128)(2,1)} %get-tuple-element.10.refs_2_, ...), custom_call_target="tpu_custom_call" | custom-call | tf_op jit(solution)/shard_map/hand_over/pallas_call | solution.py:576

commit v5 on v4

--- a/solution.py
+++ b/solution.py
@@ -424,14 +424,20 @@
     for peer in near:
         greet(peer)
 
-    for array, _ in order:
-        fetches[array].wait()
+    def prepare(array):
+        fetches.pop(array).wait()
         for m in range(H // 2):
             tile = slice(128 * m, 128 * m + 128)
             low, high = swap_halves(staged[array, 0, :, tile], staged[array, 1, :, tile])
             rep[array, 2 * m] = low
             rep[array, 2 * m + 1] = high
 
+    def in_send(unit, name, t):
+        if 2 * name + t in fetches:
+            prepare(2 * name + t)
+        unit.in_send(name, t)
+
+    prepare(0)
     alone = (lax.rem(net.z // 2 + net.z, NX) == net.x).astype(jnp.int32)
     pl.semaphore_wait(barrier, len(near) + NZ - alone)
 
@@ -443,31 +449,31 @@
         unit.in_wait(1, t)
         unit.swap_start(t)
 
-    big.in_send(0, 0)
-    small.in_send(1, 0)
-    small.in_send(0, 0)
-    big.in_send(1, 0)
-    small.in_send(0, 1)
+    in_send(big, 0, 0)
+    in_send(small, 0, 0)
+    in_send(small, 1, 0)
+    in_send(big, 1, 0)
+    in_send(small, 0, 1)
     ring_start(small, 0)
     ring_start(big, 0)
     ring_start(small, 1)
     small.ring_step(0, 1)
-    small.in_send(1, 1)
-    big.in_send(0, 1)
+    in_send(small, 1, 1)
+    in_send(big, 0, 1)
     swap_start(big, 0)
     big.ring_step(0, 1)
     swap_start(small, 0)
-    swap_start(small, 1)
     small.ring_step(0, 2)
     small.ring_step(1, 1)
+    swap_start(small, 1)
     big.ring_step(0, 2)
     big.s_compute(0)
+    ring_start(big, 1)
     small.ring_step(0, 3)
-    big.in_send(1, 1)
+    in_send(big, 1, 1)
     big.s_core(0)
     small.ring_step(0, 4)
     small.s_compute(0)
-    ring_start(big, 1)
     small.ring_step(1, 2)
     small.s_core(0)
     big.s_reduce(0)

time: 84.4 us -> 83.8 us (level)
  no operation moved by 1% of the time
where the time goes in v5:
time: 83.8 us; the launch traced here: 83.2 us
  Pallas kernels  82.6 us (99%)
    pallas_call x1, Pallas kernels, shards(): pl.pallas_call(functools.partial(kernel, factor), out_shape=(jax.ShapeDty...  80.6 us
    pallas_call x1, Pallas kernels, shards(): pl.pallas_call(hand_over, out_shape=(jax.ShapeDtypeStruct(shape, BF),) *...  1.97 us

profile of v5, /device:TPU:8, one launch (start us, length us, event | category | flops | bytes accessed | tf_op | source)
XLA Modules:
  0.0 83.2 jit_solution(9974853186261564978)
XLA Ops:
  0.6 80.6 %exchange_and_compute.1 = (bf16[2,64,768]{2,1,0:T(8,128)(2,1)}, bf16[2,64,768]{2,1,0:T(8,128)(2,1)}, bf16[2,64,768]{2,1,0:T(8,128)(2,1)}, bf16[2,64,768]{2,1,0:T(8,128)(2,1)}) custom-call(bf16[2,64,768]{2,1,0:T(8,128)(2,1)} %q_ref.1, bf16[2,64,768]{2,1,0:T(8,128)(2,1)} %k_ref.1, bf16[2,64,768]{2,1,0:T(8,128)(2,1)} %v_ref.1, bf16[2,64,768]{2,1,0:T(8,128)(2,1)} %g_ref.1), custom_call_target="tpu_custom_call" | custom-call | flops 1208000000 | bytes 1600000 | tf_op jit(solution)/shard_map/exchange_and_compute/pallas_call | solution.py:560
  81.3 2.0 %hand_over.1 = (bf16[2,64,768]{2,1,0:T(8,128)(2,1)}, bf16[2,64,768]{2,1,0:T(8,128)(2,1)}, bf16[2,64,768]{2,1,0:T(8,128)(2,1)}, bf16[2,64,768]{2,1,0:T(8,128)(2,1)}) custom-call(bf16[2,64,768]{2,1,0:T(8,128)(2,1)} %get-tuple-element.8.refs_0_, bf16[2,64,768]{2,1,0:T(8,128)(2,1)} %get-tuple-element.9.refs_1_, bf16[2,64,768]{2,1,0:T(8,128)(2,1)} %get-tuple-element.10.refs_2_, ...), custom_call_target="tpu_custom_call" | custom-call | tf_op jit(solution)/shard_map/hand_over/pallas_call | solution.py:582

commit v6 on v5

--- a/solution.py
+++ b/solution.py
@@ -304,19 +304,20 @@
         self.net.wait_recv(block, self.arrive[name, t])
 
     def out_send(self, index):
+        self.leave[index] = self.net.take()
+
+    def out_part(self, index, part):
         net = self.net
         pair = lax.rem(net.x - net.z + NZ, NX)
-        recv = net.take()
-        for k in (2, 1, 3, 0):
-            for s in range(2):
-                z_to = pair * 2 + s
-                net.remote(
-                    self.fin.at[index, pl.ds(s * C, C), net.lanes(net.xs[k])],
-                    net.orep.at[index, net.z],
-                    net.device(x=net.xs[k], z=z_to),
-                    recv=recv, alone=None if k else z_to == net.z, key=("out", s),
-                )
-        self.leave[index] = recv
+        k = (2, 1, 3, 0)[part]
+        for s in range(2):
+            z_to = pair * 2 + s
+            net.remote(
+                self.fin.at[index, pl.ds(s * C, C), net.lanes(net.xs[k])],
+                net.orep.at[index, net.z],
+                net.device(x=net.xs[k], z=z_to),
+                recv=self.leave[index], alone=None if k else z_to == net.z, key=("out", s),
+            )
 
     def out_wait(self, index):
         self.net.wait_recv(self.net.orep.at[index, pl.ds(0, NZ)], self.leave[index])
@@ -504,24 +505,40 @@
     big.edge_start(0)
     small.rs_send(1, 2)
     big.rs_end(0)
+    big.out_part(3, 0)
+    big.out_part(3, 1)
     big.p_forward(1)
-    small.rs_send(1, 3)
+    big.out_part(3, 2)
+    big.out_part(3, 3)
     big.out_compute(1)
     big.edge_start(1)
+    small.rs_send(1, 3)
     small.edge_start(0)
     big.edge_end(0)
+    big.out_part(0, 0)
+    big.out_part(0, 1)
     big.rs_send(1, 2)
+    big.out_part(0, 2)
+    big.out_part(0, 3)
     small.rs_send(1, 4)
     small.edge_start(1)
     big.edge_end(1)
+    big.out_part(1, 0)
+    big.out_part(1, 1)
+    big.out_part(1, 2)
+    big.out_part(1, 3)
     big.rs_end(1)
+    big.out_part(2, 0)
+    big.out_part(2, 1)
+    big.out_part(2, 2)
+    big.out_part(2, 3)
     small.rs_end(1)
     small.edge_end(1)
     small.edge_end(0)
     small.rs_end(0)
 
     stores = []
-    for index, ref in ((0, a_out), (1, gq_out), (3, gv_out), (2, gk_out)):
+    for index, ref in ((0, a_out), (3, gv_out), (1, gq_out), (2, gk_out)):
         big.out_wait(index)
         small.out_wait(index)
         for m in range(H // 2):

time: 83.8 us -> 83.8 us (level)
  no operation moved by 1% of the time
where the time goes in v6:
time: 83.8 us; the launch traced here: 82.5 us
  Pallas kernels  81.9 us (98%)
    pallas_call x1, Pallas kernels, shards(): pl.pallas_call(functools.partial(kernel, factor), out_shape=(jax.ShapeDty...  79.9 us
    pallas_call x1, Pallas kernels, shards(): pl.pallas_call(hand_over, out_shape=(jax.ShapeDtypeStruct(shape, BF),) *...  1.97 us

profile of v6, /device:TPU:8, one launch (start us, length us, event | category | flops | bytes accessed | tf_op | source)
XLA Modules:
  0.0 82.5 jit_solution(1058549378109675857)
XLA Ops:
  0.6 79.9 %exchange_and_compute.1 = (bf16[2,64,768]{2,1,0:T(8,128)(2,1)}, bf16[2,64,768]{2,1,0:T(8,128)(2,1)}, bf16[2,64,768]{2,1,0:T(8,128)(2,1)}, bf16[2,64,768]{2,1,0:T(8,128)(2,1)}) custom-call(bf16[2,64,768]{2,1,0:T(8,128)(2,1)} %q_ref.1, bf16[2,64,768]{2,1,0:T(8,128)(2,1)} %k_ref.1, bf16[2,64,768]{2,1,0:T(8,128)(2,1)} %v_ref.1, bf16[2,64,768]{2,1,0:T(8,128)(2,1)} %g_ref.1), custom_call_target="tpu_custom_call" | custom-call | flops 1208000000 | bytes 1600000 | tf_op jit(solution)/shard_map/exchange_and_compute/pallas_call | solution.py:577
  80.5 2.0 %hand_over.1 = (bf16[2,64,768]{2,1,0:T(8,128)(2,1)}, bf16[2,64,768]{2,1,0:T(8,128)(2,1)}, bf16[2,64,768]{2,1,0:T(8,128)(2,1)}, bf16[2,64,768]{2,1,0:T(8,128)(2,1)}) custom-call(bf16[2,64,768]{2,1,0:T(8,128)(2,1)} %get-tuple-element.8.refs_0_, bf16[2,64,768]{2,1,0:T(8,128)(2,1)} %get-tuple-element.9.refs_1_, bf16[2,64,768]{2,1,0:T(8,128)(2,1)} %get-tuple-element.10.refs_2_, ...), custom_call_target="tpu_custom_call" | custom-call | tf_op jit(solution)/shard_map/hand_over/pallas_call | solution.py:599
